TPU v7x, 128 devices: a whole 4x4x4 slice. The times are simulated.
128 devices in a mesh: level: 4 (over x), dom: 32 (over z, y, core).
Axes of the slice: x: 4, y: 4, z: 4, core: 2. Of those that a mesh axis runs over, the one named last changes fastest.
Arguments:
- rhs: float32 [4, 32, 4, 64, 1024], P('level', 'dom'), may hold values from -6 to 6
- dinv: bfloat16 [4, 32, 4, 64, 4096], P('level', 'dom'), may hold values from -0.75 to 0.75
- lower_local: bfloat16 [4, 32, 3, 64, 3, 4096], P('level', 'dom'), may hold values from -0.41992188 to 0.41992188
- lower_nbrs: int32 [4, 32, 3, 64, 3], P('level', 'dom'), may hold values from 0 to 63
- upper_local: bfloat16 [4, 32, 3, 64, 3, 4096], P('level', 'dom'), may hold values from -0.41992188 to 0.41992188
- upper_nbrs: int32 [4, 32, 3, 64, 3], P('level', 'dom'), may hold values from 0 to 63
- lower_remote: bfloat16 [4, 32, 64, 3, 4096], P('level', 'dom'), may hold values from -0.59765625 to 0.59765625
- upper_remote: bfloat16 [4, 32, 64, 3, 4096], P('level', 'dom'), may hold values from -0.59765625 to 0.59765625
- remote_slots: int32 [4, 32, 64, 3], P('level', 'dom'), may hold values from 0 to 127
- send_list: int32 [4, 32, 32, 4], P('level', 'dom'), may hold values from 0 to 63
Outputs:
- preconditioned: bfloat16 [4, 32, 4, 64, 1024], P('level', 'dom')
Inputs may be any that keep to these rules, and one draw needn't show every extreme that they name: `send_list`: A block may be listed several times.
All inputs are finite; a program needn't handle non-finite values.
Results may differ from a plain program's by a relative error of at most 0.04.
Values may be sent and summed in bfloat16 or wider, within the bound.
A program may use at most 192 MiB of HBM per device.

v0:
```python
import jax
import jax.numpy as jnp
from jax import lax
from jax.sharding import PartitionSpec as P

BS = 64


HIGHEST_PRECISION = lax.Precision.HIGHEST


def from_behind(block, axis, distance):
    devices = range(lax.axis_size(axis))
    route = [(i - distance, i) for i in devices if i - distance in devices]
    return lax.ppermute(block, axis, route)


def select_rows(selector, table):
    return jnp.dot(selector, table, preferred_element_type=jnp.float32).astype(table.dtype)


def block_product(matrices, vectors_in, count):
    mat_full = matrices.reshape(matrices.shape[0], BS, BS)
    vec_full = vectors_in.reshape(vectors_in.shape[0], count, BS)
    result = lax.dot_general(
        vec_full, mat_full, (((2,), (2,)), ((0,), (0,))), preferred_element_type=jnp.float32
    )
    return result.reshape(result.shape[0], count * BS)


def coupled_sum(matrices, selectors, table, count):
    total = None
    for couple in range(matrices.shape[1]):
        rows = select_rows(selectors[couple], table)
        term = block_product(matrices[:, couple], rows, count)
        total = term if total is None else total + term
    return total


def make_selectors(index, width):
    return (
        jnp.transpose(index)[:, :, None] == jnp.arange(width, dtype=jnp.int32)[None, None, :]
    ).astype(jnp.bfloat16)


def forward_colors(
    right_side, received, lower_local, lower_select, lower_remote, remote_select, count
):
    columns = [
        (right_side[0] - coupled_sum(lower_remote, remote_select, received, count)).astype(
            jnp.bfloat16
        )
    ]
    for color_index in range(1, right_side.shape[0]):
        columns.append(
            (
                right_side[color_index]
                - coupled_sum(
                    lower_local[color_index - 1], lower_select[color_index - 1], columns[-1], count
                )
            ).astype(jnp.bfloat16)
        )
    return jnp.stack(columns)


def backward_colors(solved, upward, dinv, upper_local, upper_select, count):
    colors = solved.shape[0]
    columns = [None] * colors
    top_rows = (solved[colors - 1].astype(jnp.float32) - upward).astype(jnp.bfloat16)
    columns[colors - 1] = block_product(dinv[colors - 1], top_rows, count).astype(jnp.bfloat16)
    for color_index in range(colors - 2, -1, -1):
        reduced = (
            solved[color_index].astype(jnp.float32)
            - coupled_sum(
                upper_local[color_index], upper_select[color_index], columns[color_index + 1], count
            )
        ).astype(jnp.bfloat16)
        columns[color_index] = block_product(dinv[color_index], reduced, count).astype(jnp.bfloat16)
    return jnp.stack(columns)


def edge_sums(leading, upper_remote, edge_select, count):
    total = None
    for couple in range(upper_remote.shape[1]):
        terms = block_product(upper_remote[:, couple], leading, count)
        part_sum = jnp.dot(
            edge_select[couple],
            terms,
            precision=HIGHEST_PRECISION,
            preferred_element_type=jnp.float32,
        )
        total = part_sum if total is None else total + part_sum
    return total


def per_device(
    rhs,
    dinv,
    lower_local,
    lower_nbrs,
    upper_local,
    upper_nbrs,
    lower_remote,
    upper_remote,
    remote_slots,
    send_list,
):
    right_side = rhs[0, 0]
    inverses = dinv[0, 0]
    lower_blocks = lower_local[0, 0]
    lower_index = lower_nbrs[0, 0]
    upper_blocks = upper_local[0, 0]
    upper_index = upper_nbrs[0, 0]
    lower_far = lower_remote[0, 0]
    upper_far = upper_remote[0, 0]
    slot_index = remote_slots[0, 0]
    send_rows = send_list[0, 0]
    levels = lax.axis_size("level")
    colors, blocks, features = right_side.shape
    vectors = features // BS
    partitions, per_peer = send_rows.shape
    slot_count = partitions * per_peer
    lower_select = [
        make_selectors(lower_index[color_index], blocks) for color_index in range(colors - 1)
    ]
    upper_select = [
        make_selectors(upper_index[color_index], blocks) for color_index in range(colors - 1)
    ]
    remote_select = make_selectors(slot_index, slot_count)
    edge_select = jnp.transpose(remote_select, (0, 2, 1)).astype(jnp.float32)
    send_select = (
        send_rows.reshape(slot_count)[:, None] == jnp.arange(blocks, dtype=jnp.int32)[None, :]
    ).astype(jnp.bfloat16)
    owner_onehot = jnp.transpose(send_select).astype(jnp.float32)
    received = jnp.zeros((slot_count, features), jnp.bfloat16)
    solved = None
    for section_num in range(levels):
        solved = forward_colors(
            right_side, received, lower_blocks, lower_select, lower_far, remote_select, vectors
        )
        if section_num + 1 < levels:
            outgoing = select_rows(send_select, solved[colors - 1]).reshape(
                partitions, per_peer, features
            )
            arrived = lax.all_to_all(outgoing, "dom", split_axis=0, concat_axis=0, tiled=True)
            received = from_behind(arrived.reshape(slot_count, features), "level", 1)
    upward = jnp.zeros((blocks, features), jnp.float32)
    answer = None
    for section_num in range(levels):
        answer = backward_colors(solved, upward, inverses, upper_blocks, upper_select, vectors)
        if section_num + 1 < levels:
            slot_sums = edge_sums(answer[0], upper_far, edge_select, vectors).reshape(
                partitions, per_peer, features
            )
            returned = lax.all_to_all(
                slot_sums.astype(jnp.bfloat16), "dom", split_axis=0, concat_axis=0, tiled=True
            ).astype(slot_sums.dtype)
            lowered = from_behind(returned.astype(jnp.bfloat16), "level", -1).astype(returned.dtype)
            upward = jnp.dot(
                owner_onehot,
                lowered.reshape(slot_count, features),
                precision=HIGHEST_PRECISION,
                preferred_element_type=jnp.float32,
            )
    return answer[None, None]


def solution(mesh):
    return jax.shard_map(
        per_device,
        mesh=mesh,
        in_specs=(
            P("level", "dom", None, None, None),
            P("level", "dom", None, None, None),
            P("level", "dom", None, None, None, None),
            P("level", "dom", None, None, None),
            P("level", "dom", None, None, None, None),
            P("level", "dom", None, None, None),
            P("level", "dom", None, None, None),
            P("level", "dom", None, None, None),
            P("level", "dom", None, None),
            P("level", "dom", None, None),
        ),
        out_specs=P("level", "dom", None, None, None),
        check_vma=False,
    )
```

profile of v0, /device:TPU:1, one launch (start us, length us, event | category | flops | bytes accessed | tf_op | source)
XLA Modules:
  0.0 763.9 jit_solution(8370022807699458815)
XLA Ops:
  8.7 2.6 reshape_squeeze.58
  19.2 4.6 slice_bitcast_fusion.3
  41.3 3.5 fusion.84
  48.9 2.8 reshape_squeeze.63
  53.4 2.9 reshape_squeeze.64
  66.2 2.8 reshape_squeeze.65
  70.8 2.7 reshape_squeeze.66
  75.4 2.8 reshape_squeeze.67
  88.0 9.6 %all-to-all-start = ((bf16[32,4,1024]{2,1,0:T(4,128)(2,1)}), bf16[32,4,1024]{2,1,0:T(4,128)(2,1)S(1)}, u32[]{:S(2)}, u32[]{:S(2)}) async-start(bf16[32,4,1024]{2,1,0:T(4,128)(2,1)} %reshape.1051), calls=%async_computation | async-start | bytes 524288 | tf_op jit(solution)/shard_map/all_to_all | solution.py:145
  97.6 4.0 slice_bitcast_fusion
  107.3 3.3 collective-permute-start
  110.7 2.6 fusion.83
  113.2 3.0 collective-permute-done
  162.9 2.7 fusion.98
  177.0 7.3 all-to-all-start.1
  184.3 2.6 fusion.80
  186.9 6.3 all-to-all-done.1
  194.0 4.4 collective-permute-start.1
  198.4 5.3 collective-permute-done.1
  252.5 4.6 all-to-all-start.2
  258.5 7.6 all-to-all-done.2
  266.9 4.0 collective-permute-start.2
  296.5 2.8 reshape_squeeze.78
  299.3 2.7 reshape_squeeze.79
  302.0 2.7 reshape_squeeze.80
  304.8 2.8 reshape_squeeze.81
  307.6 2.7 reshape_squeeze.82
  310.3 3.2 reshape_squeeze.83
  392.8 3.8 convolution_convert_fusion.14
  410.9 3.9 convolution_convert_fusion.13
  429.2 3.7 convolution_convert_fusion.12
  432.9 2.8 fusion.110
  437.5 2.8 fusion.111
  442.2 2.8 fusion.112
  452.4 13.7 %all_to_all.30 = bf16[32,4,1024]{2,1,0:T(4,128)(2,1)} all-to-all(bf16[32,4,1024]{2,1,0:T(4,128)(2,1)} %convert_element_type.779), channel_id=1, replica_groups=mesh['level'=4,'dom'=32] {'dom'}, dimensions={0} | all-to-all | bytes 524288 | tf_op jit(solution)/shard_map/all_to_all | solution.py:155
  470.4 5.6 collective-permute-done.3
  481.5 2.7 convolution_convert_fusion.11
  499.0 2.9 convolution_add_fusion.17
  501.9 3.7 convolution_convert_fusion.10
  520.5 2.9 convolution_add_fusion.15
  523.4 3.7 convolution_convert_fusion.9
  542.0 2.9 convolution_add_fusion.13
  544.9 3.7 convolution_convert_fusion.8
  548.6 2.9 fusion.118
  551.5 2.7 fusion.117
  567.6 13.6 %all_to_all.31 = bf16[32,4,1024]{2,1,0:T(4,128)(2,1)S(1)} all-to-all(bf16[32,4,1024]{2,1,0:T(4,128)(2,1)} %convert_element_type.801), channel_id=1, replica_groups=mesh['level'=4,'dom'=32] {'dom'}, dimensions={0} | all-to-all | bytes 524288 | tf_op jit(solution)/shard_map/all_to_all | solution.py:155
  582.6 8.2 %collective-permute-done.4 = bf16[32,4,1024]{2,1,0:T(4,128)(2,1)} collective-permute-done((bf16[32,4,1024]{2,1,0:T(4,128)(2,1)S(1)}, bf16[32,4,1024]{2,1,0:T(4,128)(2,1)}, u32[]{:S(2)}, u32[]{:S(2)}) %collective-permute-start.4) | collective-permute-done | bytes 262176 | tf_op jit(solution)/shard_map/ppermute | solution.py:15
  596.2 2.7 convolution_convert_fusion.7
  613.8 2.9 convolution_add_fusion.11
  616.7 3.7 convolution_convert_fusion.6
  635.3 2.9 convolution_add_fusion.9
  638.2 3.7 convolution_convert_fusion.5
  656.8 2.9 convolution_add_fusion.7
  659.7 3.7 convolution_convert_fusion.4
  663.4 2.9 fusion.124
  666.3 2.7 fusion.123
  682.4 13.6 %all_to_all.32 = bf16[32,4,1024]{2,1,0:T(4,128)(2,1)S(1)} all-to-all(bf16[32,4,1024]{2,1,0:T(4,128)(2,1)} %convert_element_type.823), channel_id=1, replica_groups=mesh['level'=4,'dom'=32] {'dom'}, dimensions={0} | all-to-all | bytes 524288 | tf_op jit(solution)/shard_map/all_to_all | solution.py:155
  697.5 8.1 %collective-permute-done.5 = bf16[32,4,1024]{2,1,0:T(4,128)(2,1)} collective-permute-done((bf16[32,4,1024]{2,1,0:T(4,128)(2,1)S(1)}, bf16[32,4,1024]{2,1,0:T(4,128)(2,1)}, u32[]{:S(2)}, u32[]{:S(2)}) %collective-permute-start.5) | collective-permute-done | bytes 262176 | tf_op jit(solution)/shard_map/ppermute | solution.py:15
  711.0 2.7 convolution_convert_fusion.3
  726.4 2.9 convolution_add_fusion.5
  729.3 3.5 convolution_convert_fusion.2
  740.3 2.9 convolution_add_fusion.3
  743.2 3.1 convolution_convert_fusion.1
  757.4 2.6 convolution_add_fusion.1
  (567 shorter events, 497.3 us)
Async XLA Ops:
  7.6 4.3 copy-start.15
  13.3 2.6 copy-start.98
  13.3 2.8 copy-start.38
  25.8 197.1 %copy-start = (bf16[64,64,64]{2,1,0:T(8,128)(2,1)}, bf16[64,64,64]{2,1,0:T(8,128)(2,1)S(1)}, u32[]{:S(2)}) copy-start(bf16[64,64,64]{2,1,0:T(8,128)(2,1)S(1)} %reshape_squeeze.59) | copy-start | bytes 1572868
  25.8 4.2 copy-start.89
  46.9 186.9 %copy-start.3 = (bf16[64,64,64]{2,1,0:T(8,128)(2,1)}, bf16[64,64,64]{2,1,0:T(8,128)(2,1)S(1)}, u32[]{:S(2)}) copy-start(bf16[64,64,64]{2,1,0:T(8,128)(2,1)S(1)} %reshape_squeeze.62) | copy-start | bytes 1572868
  81.5 2.6 copy-start.100
  88.0 18.5 %all-to-all-start = ((bf16[32,4,1024]{2,1,0:T(4,128)(2,1)}), bf16[32,4,1024]{2,1,0:T(4,128)(2,1)S(1)}, u32[]{:S(2)}, u32[]{:S(2)}) async-start(bf16[32,4,1024]{2,1,0:T(4,128)(2,1)} %reshape.1051), calls=%async_computation | async-start | bytes 524288 | tf_op jit(solution)/shard_map/all_to_all | solution.py:145
  101.7 2.7 copy-start.48
  107.3 8.9 %collective-permute-start = (bf16[128,1024]{1,0:T(8,128)(2,1)}, bf16[128,1024]{1,0:T(8,128)(2,1)S(1)}, u32[]{:S(2)}, u32[]{:S(2)}) collective-permute-start(bf16[128,1024]{1,0:T(8,128)(2,1)} %reshape.1052), channel_id=1, source_target_pairs={{0,32},{32,64},{64,96},{1,33},{33,65},{65,97},{2,34},{34,66},{66,9... | collective-permute-start | bytes 786440 | tf_op jit(solution)/shard_map/ppermute | solution.py:15
  177.0 16.2 %all-to-all-start.1 = ((bf16[32,4,1024]{2,1,0:T(4,128)(2,1)}), bf16[32,4,1024]{2,1,0:T(4,128)(2,1)S(1)}, u32[]{:S(2)}, u32[]{:S(2)}) async-start(bf16[32,4,1024]{2,1,0:T(4,128)(2,1)} %reshape.1065), calls=%async_computation.1 | async-start | bytes 524288 | tf_op jit(solution)/shard_map/all_to_all | solution.py:145
  184.3 14.1 %copy-start.99 = (s32[1,1,3,64,3]{3,1,4,2,0:T(1,128)S(1)}, s32[1,1,3,64,3]{3,1,4,2,0:T(1,128)}, u32[]{:S(2)}) copy-start(s32[1,1,3,64,3]{3,1,4,2,0:T(1,128)} %param.15) | copy-start | bytes 6916
  194.0 9.8 %collective-permute-start.1 = (bf16[128,1024]{1,0:T(8,128)(2,1)}, bf16[128,1024]{1,0:T(8,128)(2,1)S(1)}, u32[]{:S(2)}, u32[]{:S(2)}) collective-permute-start(bf16[128,1024]{1,0:T(8,128)(2,1)} %reshape.1066), channel_id=1, source_target_pairs={{0,32},{32,64},{64,96},{1,33},{33,65},{65,97},{2,34},{34,66},{66,9... | collective-permute-start | bytes 786440 | tf_op jit(solution)/shard_map/ppermute | solution.py:15
  224.4 5.1 copy-start.21
  238.3 5.0 copy-start.5
  242.1 5.7 copy-start.32
  244.8 4.8 copy-start.35
  250.2 21.4 %copy-start.62 = (f32[1,1,1,64,1024]{4,3,2,1,0:T(8,128)S(1)}, f32[1,1,1,64,1024]{4,3,2,1,0:T(8,128)}, u32[]{:S(2)}) copy-start(f32[1,1,1,64,1024]{4,3,2,1,0:T(8,128)} %get-tuple-element.39) | copy-start | bytes 786436
  250.4 22.2 %copy-start.61 = (f32[1,1,1,64,1024]{4,3,2,1,0:T(8,128)S(1)}, f32[1,1,1,64,1024]{4,3,2,1,0:T(8,128)}, u32[]{:S(2)}) copy-start(f32[1,1,1,64,1024]{4,3,2,1,0:T(8,128)} %get-tuple-element.42) | copy-start | bytes 786436
  251.7 21.8 %copy-start.60 = (f32[1,1,1,64,1024]{4,3,2,1,0:T(8,128)S(1)}, f32[1,1,1,64,1024]{4,3,2,1,0:T(8,128)}, u32[]{:S(2)}) copy-start(f32[1,1,1,64,1024]{4,3,2,1,0:T(8,128)} %get-tuple-element.43) | copy-start | bytes 786436
  252.5 13.6 %all-to-all-start.2 = ((bf16[32,4,1024]{2,1,0:T(4,128)(2,1)}), bf16[32,4,1024]{2,1,0:T(4,128)(2,1)S(1)}, u32[]{:S(2)}, u32[]{:S(2)}) async-start(bf16[32,4,1024]{2,1,0:T(4,128)(2,1)} %reshape.1079), calls=%async_computation.2 | async-start | bytes 524288 | tf_op jit(solution)/shard_map/all_to_all | solution.py:145
  257.1 17.4 %copy-start.59 = (f32[1,1,1,64,1024]{4,3,2,1,0:T(8,128)S(1)}, f32[1,1,1,64,1024]{4,3,2,1,0:T(8,128)}, u32[]{:S(2)}) copy-start(f32[1,1,1,64,1024]{4,3,2,1,0:T(8,128)} %get-tuple-element.41) | copy-start | bytes 786436
  266.9 47.3 %collective-permute-start.2 = (bf16[128,1024]{1,0:T(8,128)(2,1)}, bf16[128,1024]{1,0:T(8,128)(2,1)S(1)}, u32[]{:S(2)}, u32[]{:S(2)}) collective-permute-start(bf16[128,1024]{1,0:T(8,128)(2,1)} %reshape.1080), channel_id=1, source_target_pairs={{0,32},{32,64},{64,96},{1,33},{33,65},{65,97},{2,34},{34,66},{66,9... | collective-permute-start | bytes 786440 | tf_op jit(solution)/shard_map/ppermute | solution.py:15
  271.6 3.8 copy-start.58
  273.5 4.0 copy-start.51
  275.4 4.2 copy-start.50
  277.5 4.2 copy-start.49
  279.6 4.2 copy-start.57
  283.7 4.4 copy-start.47
  285.9 4.4 copy-start.46
  320.3 4.8 copy-start.14
  326.5 7.3 copy-start.1
  336.3 5.9 copy-start.22
  343.7 7.3 copy-start.4
  353.4 5.9 copy-start.29
  360.8 7.4 copy-start.6
  366.3 6.2 copy-start.92
  370.6 5.0 copy-start.36
  378.4 11.2 %copy-start.2 = (bf16[64,64,64]{2,1,0:T(8,128)(2,1)S(1)}, bf16[64,64,64]{2,1,0:T(8,128)(2,1)}, u32[]{:S(2)}) copy-start(bf16[64,64,64]{2,1,0:T(8,128)(2,1)} %reshape_squeeze.69) | copy-start | bytes 1572868
  440.3 6.6 copy-start.86
  446.9 2.7 copy-start.85
  466.2 9.9 %collective-permute-start.3 = (bf16[32,4,1024]{2,1,0:T(4,128)(2,1)}, bf16[32,4,1024]{2,1,0:T(4,128)(2,1)}, u32[]{:S(2)}, u32[]{:S(2)}) collective-permute-start(bf16[32,4,1024]{2,1,0:T(4,128)(2,1)} %all_to_all.30), channel_id=1, source_target_pairs={{32,0},{64,32},{96,64},{33,1},{65,33},{97,65},{34,2},{66,34},{98,6... | collective-permute-start | bytes 786440 | tf_op jit(solution)/shard_map/ppermute | solution.py:15
  548.6 2.9 copy-start.43
  548.6 5.6 copy-start.39
  561.3 2.7 copy-start.84
  581.1 9.7 %collective-permute-start.4 = (bf16[32,4,1024]{2,1,0:T(4,128)(2,1)S(1)}, bf16[32,4,1024]{2,1,0:T(4,128)(2,1)}, u32[]{:S(2)}, u32[]{:S(2)}) collective-permute-start(bf16[32,4,1024]{2,1,0:T(4,128)(2,1)S(1)} %all_to_all.31), channel_id=1, source_target_pairs={{32,0},{64,32},{96,64},{33,1},{65,33},{97,65},{34,2},{66,34},{98,6... | collective-permute-start | bytes 786440 | tf_op jit(solution)/shard_map/ppermute | solution.py:15
  663.4 2.9 copy-start.42
  663.4 5.6 copy-start.40
  676.1 2.7 copy-start.83
  695.9 9.7 %collective-permute-start.5 = (bf16[32,4,1024]{2,1,0:T(4,128)(2,1)S(1)}, bf16[32,4,1024]{2,1,0:T(4,128)(2,1)}, u32[]{:S(2)}, u32[]{:S(2)}) collective-permute-start(bf16[32,4,1024]{2,1,0:T(4,128)(2,1)S(1)} %all_to_all.32), channel_id=1, source_target_pairs={{32,0},{64,32},{96,64},{33,1},{65,33},{97,65},{34,2},{66,34},{98,6... | collective-permute-start | bytes 786440 | tf_op jit(solution)/shard_map/ppermute | solution.py:15
  719.3 6.2 copy-start.93
  723.6 5.7 copy-start.24
  729.3 4.6 copy-start.88
  735.7 3.6 copy-start.94
  737.4 5.8 copy-start.16
  737.4 5.8 copy-start.17
  743.2 4.3 copy-start.87
  746.3 4.9 copy-start.45
  746.3 5.7 copy-start.44
  752.0 4.5 copy-start.90
  752.9 4.5 copy-start.9
  754.5 5.5 copy-start.7
  754.5 5.5 copy-start.10
  760.0 2.6 copy-start.96
  (46 other events, 83.4 us)
where the time goes:
time: 774 us; the launch traced here: 764 us
  matrix products  317 us (41%)
  local copies, waits for them, and re-layouts  305 us (39%)
  waiting for transfers between devices  44.9 us (6%)
  blocking collectives  40.9 us (5%)
  starting transfers between devices  37.5 us (5%)
  other arithmetic  17.2 us (2%)
    dot_general x97, matrix products, block_product(): lax.dot_general(vec_full, mat_full, (((2,), (2,)), ((0,), (0,))), preferr...  206 us
    reshape x87, local copies, waits for them, and re-layouts, block_product(): vec_full = vectors_in.reshape(vectors_in.shape[0], count, BS)  131 us
    dot_general x87, matrix products, select_rows(): jnp.dot(selector, table, preferred_element_type=jnp.float32)  92.6 us
    another operation x28, local copies, waits for them, and re-layouts, block_product(): mat_full = matrices.reshape(matrices.shape[0], BS, BS)  64.2 us
    all_to_all x3, blocking collectives, per_device(): lax.all_to_all(slot_sums.astype(jnp.bfloat16), 'dom', split_axis=0, conca...  40.9 us
    ppermute x6, waiting for transfers between devices, from_behind(): return lax.ppermute(block, axis, route)  30.2 us
    all_to_all x3, starting transfers between devices, per_device(): lax.all_to_all(outgoing, 'dom', split_axis=0, concat_axis=0, tiled=True)  21.4 us
    add x16, local copies, waits for them, and re-layouts, coupled_sum(): total = term if total is None else total + term  20 us
  transfers between devices with their start and end apart: 9, of which 8 were waited for; matrix products, arithmetic and copies ran while one was open for 8% of the time, Pallas kernels for 0%

commit v1 on v0

v1 whole, which is shorter than its diff:
```python
import functools

import jax
import jax.numpy as jnp
from jax import lax
from jax.experimental import pallas as pl
from jax.experimental.pallas import tpu as pltpu
from jax.sharding import PartitionSpec as P

BS = 64
GROUP = 4
MESH = pl.DeviceIdType.MESH
BF16 = jnp.bfloat16
F32 = jnp.float32


def dot_rows(left, right):
    return lax.dot_general(left, right, (((1,), (1,)), ((), ())), preferred_element_type=F32)


def kernel(
    levels,
    parts,
    low_idx,
    up_idx,
    slot_idx,
    send_idx,
    edge_code,
    owner_code,
    rhs,
    w_low,
    w_up,
    w_lrem,
    w_urem,
    w_dinv,
    out,
    solved,
    table,
    rtable,
    boundary,
    upward,
    terms,
    edge_hot,
    owner_hot,
    send_f,
    recv_f,
    send_b,
    recv_b,
    sems,
):
    level = lax.axis_index("level")
    me = lax.axis_index("dom")
    colors, blocks = solved.shape[0], solved.shape[1]
    groups = blocks // GROUP
    rows_per_peer = send_f.shape[0] // parts

    barrier = pltpu.get_barrier_semaphore()

    def greet(step, _):
        peer = lax.rem(me + step, parts)

        @pl.when(level > 0)
        def _():
            pl.semaphore_signal(barrier, inc=1, device_id=(level - 1, peer), device_id_type=MESH)

        @pl.when(level < levels - 1)
        def _():
            pl.semaphore_signal(barrier, inc=1, device_id=(level + 1, peer), device_id_type=MESH)

        return 0

    lax.fori_loop(0, parts, greet, 0)

    low_half16 = lax.broadcasted_iota(jnp.int32, (16, 128), 1) < BS
    low_half8 = lax.broadcasted_iota(jnp.int32, (8, 128), 1) < BS
    zero16 = jnp.zeros((16, 128), F32)

    def doubled(packed):
        turned = pltpu.roll(packed, BS, 1)
        return jnp.concatenate(
            [jnp.where(low_half8, packed, turned), jnp.where(low_half8, turned, packed)], axis=0
        )

    def paired(rows):
        return jnp.where(low_half8, rows[:8], rows[8:])

    def gathered(idx, base, source, group):
        pieces = []
        for member in range(GROUP):
            at = base + (group * GROUP + member) * 3
            first, second, third = source[idx[at]], source[idx[at + 1]], source[idx[at + 2]]
            pieces.append(
                jnp.concatenate([jnp.where(low_half16, first, second), third], axis=1)
            )
        return jnp.concatenate(pieces, axis=0)

    def own_block(product, member):
        piece = product[member * 16 : member * 16 + 16, (member // 2) * 128 : (member // 2) * 128 + 128]
        turned = pltpu.roll(piece, BS, 1)
        return jnp.where(low_half16, piece, turned) if member % 2 == 0 else jnp.where(low_half16, turned, piece)

    def spread(members):
        pieces = []
        for member, value in enumerate(members):
            kept = jnp.where(low_half16, value, zero16) if member % 2 == 0 else jnp.where(low_half16, zero16, value)
            pair = [kept, zero16] if member < 2 else [zero16, kept]
            pieces.append(jnp.concatenate(pair, axis=1).astype(BF16))
        return jnp.concatenate(pieces, axis=0)

    def forward_step(weights, windex, idx, base, source, color):
        def body(group, _):
            product = dot_rows(gathered(idx, base, source, group), weights[windex + group])
            for member in range(GROUP):
                block = group * GROUP + member
                value = rhs[color, block] - own_block(product, member)
                solved[color, block] = value.astype(BF16)
            return 0

        lax.fori_loop(0, groups, body, 0, unroll=4)

    @pl.when(level == 0)
    def _():
        def body(block, _):
            solved[0, block] = rhs[0, block].astype(BF16)
            return 0

        lax.fori_loop(0, blocks, body, 0, unroll=8)

    @pl.when(level > 0)
    def _():
        pltpu.make_async_copy(recv_f, recv_f, sems.at[1]).wait()

        def body(pair, _):
            both = recv_f[pl.ds(pl.multiple_of(pair * 16, 16), 16), :].astype(F32)
            rtable[pair * 2] = doubled(both[:8]).astype(BF16)
            rtable[pair * 2 + 1] = doubled(both[8:]).astype(BF16)
            return 0

        lax.fori_loop(0, recv_f.shape[0] // 16, body, 0, unroll=8)
        forward_step(w_lrem, 0, slot_idx, 0, rtable, 0)

    def color_body(color, _):
        forward_step(w_low, (color - 1) * groups, low_idx, (color - 1) * blocks * 3, solved.at[color - 1], color)
        return 0

    lax.fori_loop(1, colors, color_body, 0)

    pl.semaphore_wait(
        barrier, parts * ((level > 0).astype(jnp.int32) + (level < levels - 1).astype(jnp.int32))
    )

    @pl.when(level < levels - 1)
    def _():
        def pack(block, _):
            boundary[block] = paired(solved[colors - 1, block].astype(F32))
            return 0

        lax.fori_loop(0, blocks, pack, 0, unroll=8)

        def body(pair, _):
            both = jnp.concatenate(
                [boundary[send_idx[pair * 2]], boundary[send_idx[pair * 2 + 1]]], axis=0
            )
            send_f[pl.ds(pl.multiple_of(pair * 16, 16), 16), :] = both.astype(BF16)
            return 0

        lax.fori_loop(0, send_f.shape[0] // 16, body, 0, unroll=8)

        def push(step, _):
            peer = lax.rem(me + step, parts)
            pltpu.make_async_remote_copy(
                src_ref=send_f.at[pl.ds(pl.multiple_of(peer * rows_per_peer, 16), rows_per_peer)],
                dst_ref=recv_f.at[pl.ds(pl.multiple_of(me * rows_per_peer, 16), rows_per_peer)],
                send_sem=sems.at[0],
                recv_sem=sems.at[1],
                device_id=(level + 1, peer),
                device_id_type=MESH,
            ).start()
            return 0

        lax.fori_loop(0, parts, push, 0)

    def hot_edge(chunk, _):
        rows = lax.broadcasted_iota(jnp.int32, (64, edge_hot.shape[1]), 0) + chunk * 64
        edge_hot[pl.ds(pl.multiple_of(chunk * 64, 64), 64), :] = jnp.where(
            rows == edge_code[...], 1.0, 0.0
        ).astype(BF16)
        return 0

    lax.fori_loop(0, edge_hot.shape[0] // 64, hot_edge, 0)

    def hot_owner(chunk, _):
        rows = lax.broadcasted_iota(jnp.int32, (64, owner_hot.shape[1]), 0) + chunk * 64
        owner_hot[pl.ds(pl.multiple_of(chunk * 64, 64), 64), :] = jnp.where(
            rows == owner_code[...], 1.0, 0.0
        ).astype(BF16)
        return 0

    lax.fori_loop(0, owner_hot.shape[0] // 64, hot_owner, 0)

    def finish(color, group, members):
        weights = w_dinv[color * groups + group]
        product = dot_rows(spread(members), jnp.concatenate([weights, weights], axis=0))
        outs = []
        for member in range(GROUP):
            value = product[member * 16 : member * 16 + 16]
            table[color, group * GROUP + member] = value.astype(BF16)
            outs.append(paired(value))
        out[color, pl.ds(pl.multiple_of(group * GROUP * 8, 32), GROUP * 8), :] = jnp.concatenate(
            outs, axis=0
        ).astype(BF16)

    @pl.when(level == levels - 1)
    def _():
        upward[...] = jnp.zeros_like(upward)

    @pl.when(level < levels - 1)
    def _():
        pltpu.make_async_copy(recv_b, recv_b, sems.at[3]).wait()
        upward[...] = jnp.dot(owner_hot[...], recv_b[...], preferred_element_type=F32)

    def last_color(group, _):
        members = []
        for member in range(GROUP):
            block = group * GROUP + member
            add = upward[pl.ds(pl.multiple_of(block * 8, 8), 8), :]
            members.append(solved[colors - 1, block].astype(F32) - doubled(add))
        finish(colors - 1, group, members)
        return 0

    lax.fori_loop(0, groups, last_color, 0, unroll=4)

    def back_color(step, _):
        color = colors - 2 - step
        source = table.at[color + 1]

        def body(group, _):
            product = dot_rows(
                gathered(up_idx, color * blocks * 3, source, group), w_up[color * groups + group]
            )
            members = [
                solved[color, group * GROUP + member].astype(F32) - own_block(product, member)
                for member in range(GROUP)
            ]
            finish(color, group, members)
            return 0

        lax.fori_loop(0, groups, body, 0, unroll=4)
        return 0

    lax.fori_loop(0, colors - 1, back_color, 0)

    @pl.when(level > 0)
    def _():
        def body(group, _):
            members = [table[0, group * GROUP + member].astype(F32) for member in range(GROUP)]
            product = dot_rows(spread(members), w_urem[group])
            pieces = []
            for member in range(GROUP):
                rows = product[member * 16 : member * 16 + 16]
                first, third = rows[:, :128], rows[:, 128:]
                turned = pltpu.roll(first, BS, 1)
                third_turned = pltpu.roll(third, BS, 1)
                pieces.append(jnp.where(low_half8, first[:8], turned[8:]))
                pieces.append(jnp.where(low_half8, turned[:8], first[8:]))
                pieces.append(jnp.where(low_half8, third[:8], third_turned[8:]))
            terms[pl.ds(pl.multiple_of(group * GROUP * 24, 96), GROUP * 24), :] = jnp.concatenate(
                pieces, axis=0
            ).astype(BF16)
            return 0

        lax.fori_loop(0, groups, body, 0, unroll=4)

        send_b[...] = jnp.dot(edge_hot[...], terms[...], preferred_element_type=F32).astype(BF16)

        def push(step, _):
            peer = lax.rem(me + step, parts)
            pltpu.make_async_remote_copy(
                src_ref=send_b.at[pl.ds(pl.multiple_of(peer * rows_per_peer, 16), rows_per_peer)],
                dst_ref=recv_b.at[pl.ds(pl.multiple_of(me * rows_per_peer, 16), rows_per_peer)],
                send_sem=sems.at[2],
                recv_sem=sems.at[3],
                device_id=(level - 1, peer),
                device_id_type=MESH,
            ).start()
            return 0

        lax.fori_loop(0, parts, push, 0)
        pltpu.make_async_copy(send_b, send_b, sems.at[2]).wait()

    @pl.when(level < levels - 1)
    def _():
        pltpu.make_async_copy(send_f, send_f, sems.at[0]).wait()


def per_device(
    levels,
    parts,
    rhs,
    dinv,
    lower_local,
    lower_nbrs,
    upper_local,
    upper_nbrs,
    lower_remote,
    upper_remote,
    remote_slots,
    send_list,
):
    colors, blocks, features = rhs.shape[2:]
    groups = blocks // GROUP
    slots = parts * send_list.shape[-1]

    def coupling_rows(matrices):
        count = matrices.shape[0]
        split = matrices.reshape(count, blocks, 3, BS, BS).transpose(0, 1, 3, 2, 4)
        flat = split.reshape(count * groups, GROUP * BS, 3 * BS)
        return jnp.pad(flat, ((0, 0), (0, 0), (0, BS)))

    w_low = coupling_rows(lower_local[0, 0])
    w_up = coupling_rows(upper_local[0, 0])
    w_lrem = coupling_rows(lower_remote[0])
    w_urem = (
        upper_remote[0, 0]
        .reshape(groups, GROUP, 3, BS, BS)
        .transpose(0, 2, 3, 1, 4)
        .reshape(groups, 3 * BS, GROUP * BS)
    )
    w_urem = jnp.pad(w_urem, ((0, 0), (0, BS), (0, 0)))
    w_dinv = (
        dinv[0, 0]
        .reshape(colors * groups, GROUP, BS, BS)
        .transpose(0, 2, 1, 3)
        .reshape(colors * groups, BS, GROUP * BS)
    )
    halves = rhs[0, 0].reshape(colors, blocks, 8, 2, BS).transpose(0, 1, 3, 2, 4)
    halves = halves.reshape(colors, blocks, 16, BS)
    right = jnp.concatenate([halves, halves], axis=-1)
    lanes = jnp.arange(8, dtype=jnp.int32)
    edge_code = (remote_slots.reshape(blocks * 3, 1) * 8 + lanes).reshape(1, blocks * 24)
    owner_code = (send_list.reshape(slots, 1) * 8 + lanes).reshape(1, slots * 8)

    smem = pl.BlockSpec(memory_space=pltpu.SMEM)
    vmem = pl.BlockSpec(memory_space=pltpu.VMEM)
    answer = pl.pallas_call(
        functools.partial(kernel, levels, parts),
        out_shape=jax.ShapeDtypeStruct((colors, blocks * 8, 128), BF16),
        in_specs=[smem] * 4 + [vmem] * 8,
        out_specs=vmem,
        scratch_shapes=[
            pltpu.VMEM((colors, blocks, 16, 128), BF16),
            pltpu.VMEM((colors, blocks, 16, 128), BF16),
            pltpu.VMEM((slots, 16, 128), BF16),
            pltpu.VMEM((blocks, 8, 128), F32),
            pltpu.VMEM((blocks * 8, 128), F32),
            pltpu.VMEM((blocks * 24, 128), BF16),
            pltpu.VMEM((slots * 8, blocks * 24), BF16),
            pltpu.VMEM((blocks * 8, slots * 8), BF16),
            pltpu.VMEM((slots * 8, 128), BF16),
            pltpu.VMEM((slots * 8, 128), BF16),
            pltpu.VMEM((slots * 8, 128), BF16),
            pltpu.VMEM((slots * 8, 128), BF16),
            pltpu.SemaphoreType.DMA((4,)),
        ],
        compiler_params=pltpu.CompilerParams(
            collective_id=0, has_side_effects=True, vmem_limit_bytes=60 * 1024 * 1024
        ),
        name="sweeps",
    )(
        lower_nbrs.reshape(-1),
        upper_nbrs.reshape(-1),
        remote_slots.reshape(-1),
        send_list.reshape(-1),
        edge_code,
        owner_code,
        right,
        w_low,
        w_up,
        w_lrem,
        w_urem,
        w_dinv,
    )
    return answer.reshape(1, 1, colors, blocks, features)


def solution(mesh):
    levels, parts = mesh.shape["level"], mesh.shape["dom"]
    return jax.shard_map(
        functools.partial(per_device, levels, parts),
        mesh=mesh,
        in_specs=(
            P("level", "dom", None, None, None),
            P("level", "dom", None, None, None),
            P("level", "dom", None, None, None, None),
            P("level", "dom", None, None, None),
            P("level", "dom", None, None, None, None),
            P("level", "dom", None, None, None),
            P("level", "dom", None, None, None),
            P("level", "dom", None, None, None),
            P("level", "dom", None, None),
            P("level", "dom", None, None),
        ),
        out_specs=P("level", "dom", None, None, None),
        check_vma=False,
    )
```

time: 774 us -> 379 us (0.49)
  matrix products: 317 us -> 0 us
  Pallas kernels: 0 us -> 193 us
  local copies, waits for them, and re-layouts: 305 us -> 181 us
  waiting for transfers between devices: 44.9 us -> 0 us
  blocking collectives: 40.9 us -> 0 us
  starting transfers between devices: 37.5 us -> 0 us
  other arithmetic: 17.2 us -> 2.14 us
    dot_general x196 -> x0, matrix products: 317 us -> none  [the longest x97 206 us: block_product(): lax.dot_general(vec_full, mat_full, (((2,), (2,)), ((0,), (0,))), preferr...]
    pallas_call x0 -> x1, Pallas kernels: none -> 193 us  [per_device(): pl.pallas_call(functools.partial(kernel, levels, parts), out_shape=jax.Sh...]
    reshape x105 -> x13, local copies, waits for them, and re-layouts: 160 us -> 64.8 us  [the longest x6 50.8 us: coupling_rows(): flat = split.reshape(count * groups, GROUP * BS, 3 * BS)]
    all_to_all x3 -> x0, blocking collectives: 40.9 us -> none  [per_device(): lax.all_to_all(slot_sums.astype(jnp.bfloat16), 'dom', split_axis=0, conca...]
    ppermute x6 -> x0, waiting for transfers between devices: 30.2 us -> none  [from_behind(): return lax.ppermute(block, axis, route)]
    another operation x28 -> x12, local copies, waits for them, and re-layouts: 64.2 us -> 93.8 us  [the longest x6 63.4 us: coupling_rows(): split = matrices.reshape(count, blocks, 3, BS, BS).transpose(0, 1, 3, 2, 4)]
    convert_element_type x19 -> x0, local copies, waits for them, and re-layouts: 26.8 us -> none  [the longest x11 14.7 us: backward_colors(): block_product(dinv[color_index], reduced, count).astype(jnp.bfloat16)]
    all_to_all x3 -> x0, starting transfers between devices: 21.4 us -> none  [per_device(): lax.all_to_all(outgoing, 'dom', split_axis=0, concat_axis=0, tiled=True)]
  transfers between devices with their start and end apart: 9 -> 0, of which waited for: 8 -> 0; matrix products, arithmetic and copies ran while one was open for 8% -> 0% of each run, Pallas kernels for 0% -> 0%
where the time goes in v1:
time: 379 us; the launch traced here: 376 us
  Pallas kernels  193 us (51%)
  local copies, waits for them, and re-layouts  181 us (48%)
    pallas_call x1, Pallas kernels, per_device(): pl.pallas_call(functools.partial(kernel, levels, parts), out_shape=jax.Sh...  193 us
    another operation x6, local copies, waits for them, and re-layouts, coupling_rows(): split = matrices.reshape(count, blocks, 3, BS, BS).transpose(0, 1, 3, 2, 4)  63.4 us
    reshape x6, local copies, waits for them, and re-layouts, coupling_rows(): flat = split.reshape(count * groups, GROUP * BS, 3 * BS)  50.8 us
    another operation x2, local copies, waits for them, and re-layouts, per_device(): w_dinv = dinv[0, 0].reshape(colors * groups, GROUP, BS, BS).transpose(0,...  19.4 us
    pad x3, local copies, waits for them, and re-layouts, coupling_rows(): return jnp.pad(flat, ((0, 0), (0, 0), (0, BS)))  16 us
    another operation x2, local copies, waits for them, and re-layouts, per_device(): w_urem = upper_remote[0, 0].reshape(groups, GROUP, 3, BS, BS).transpose(0...  9.34 us

profile of v1, /device:TPU:1, one launch (start us, length us, event | category | flops | bytes accessed | tf_op | source)
XLA Modules:
  0.0 375.8 jit_solution(7307928356980351108)
XLA Ops:
  0.0 0.8 copy.20
  0.8 0.1 reshape.97.slot_idx
  0.9 0.0 copy-start.3
  0.9 0.1 iota_add_fusion
  1.0 0.7 add.57.edge_code
  1.7 0.8 copy.21
  2.5 0.1 reshape.98.send_idx
  2.6 0.0 copy-start.6
  2.6 0.1 iota_add_fusion.1
  2.7 0.7 add.61.owner_code
  3.4 13.8 %reshape_squeeze.19 = bf16[3,64,3,64,64]{4,3,1,2,0:T(8,128)(2,1)} reshape(bf16[1,1,3,64,3,4096]{5,3,4,2,1,0:T(8,128)(2,1)} %param.12) | data formatting | bytes 9437184 | tf_op jit(solution)/shard_map/reshape;squeeze | solution.py:316
  17.2 0.0 copy-done.3
  17.2 0.0 copy-done.6
  17.2 13.6 %copy.23 = bf16[3,64,3,64,64]{3,1,0,4,2:T(8,128)(2,1)} copy(bf16[3,64,3,64,64]{4,3,1,2,0:T(8,128)(2,1)} %reshape_squeeze.19) | data formatting | bytes 9437184 | tf_op jit(solution)/shard_map/reshape;squeeze | solution.py:316
  30.8 13.3 %reshape.100 = bf16[48,256,192]{1,0,2:T(8,128)(2,1)} reshape(bf16[3,64,64,3,64]{2,1,0,4,3:T(8,128)(2,1)} %bitcast.54) | data formatting | bytes 9437184 | tf_op jit(solution)/shard_map/reshape | solution.py:317
  44.1 9.2 %copy.24 = bf16[48,256,192]{2,1,0:T(8,128)(2,1)} copy(bf16[48,256,192]{1,0,2:T(8,128)(2,1)} %reshape.100) | data formatting | bytes 9437184 | tf_op jit(solution)/shard_map/reshape | solution.py:317
  53.3 7.0 %pad.15.w_low = bf16[48,256,256]{2,1,0:T(8,128)(2,1)} pad(bf16[48,256,192]{2,1,0:T(8,128)(2,1)} %copy.24, bf16[]{:T(256)} %constant.1.clone.1), padding=0_0x0_0x0_64 | pad | bytes 11010050 | tf_op jit(solution)/shard_map/jit(_pad)/pad | solution.py:318
  60.4 13.8 %reshape_squeeze.20 = bf16[3,64,3,64,64]{4,3,1,2,0:T(8,128)(2,1)} reshape(bf16[1,1,3,64,3,4096]{5,3,4,2,1,0:T(8,128)(2,1)} %param.14) | data formatting | bytes 9437184 | tf_op jit(solution)/shard_map/reshape;squeeze | solution.py:316
  74.2 13.6 %copy.25 = bf16[3,64,3,64,64]{3,1,0,4,2:T(8,128)(2,1)} copy(bf16[3,64,3,64,64]{4,3,1,2,0:T(8,128)(2,1)} %reshape_squeeze.20) | data formatting | bytes 9437184 | tf_op jit(solution)/shard_map/reshape;squeeze | solution.py:316
  87.7 13.3 %reshape.101 = bf16[48,256,192]{1,0,2:T(8,128)(2,1)} reshape(bf16[3,64,64,3,64]{2,1,0,4,3:T(8,128)(2,1)} %bitcast.55) | data formatting | bytes 9437184 | tf_op jit(solution)/shard_map/reshape | solution.py:317
  101.1 9.2 %copy.26 = bf16[48,256,192]{2,1,0:T(8,128)(2,1)} copy(bf16[48,256,192]{1,0,2:T(8,128)(2,1)} %reshape.101) | data formatting | bytes 9437184 | tf_op jit(solution)/shard_map/reshape | solution.py:317
  110.3 0.0 copy-start
  110.3 7.2 %pad.16.w_up = bf16[48,256,256]{2,1,0:T(8,128)(2,1)} pad(bf16[48,256,192]{2,1,0:T(8,128)(2,1)} %copy.26, bf16[]{:T(256)} %constant.1.clone.1), padding=0_0x0_0x0_64 | pad | bytes 11010050 | tf_op jit(solution)/shard_map/jit(_pad)/pad | solution.py:318
  117.5 0.0 copy-done
  117.5 4.4 %reshape_squeeze.21 = bf16[1,64,3,64,64]{4,3,1,2,0:T(8,128)(2,1)} reshape(bf16[1,1,64,3,4096]{4,2,3,1,0:T(8,128)(2,1)S(1)} %copy-done) | data formatting | bytes 3145728 | tf_op jit(solution)/shard_map/reshape;squeeze | solution.py:316
  121.9 4.3 %copy.27 = bf16[1,64,3,64,64]{3,1,4,2,0:T(8,128)(2,1)S(1)} copy(bf16[1,64,3,64,64]{4,3,1,2,0:T(8,128)(2,1)} %reshape_squeeze.21) | data formatting | bytes 3145728 | tf_op jit(solution)/shard_map/reshape;squeeze | solution.py:316
  126.2 3.0 reshape.102
  129.1 2.8 copy.28
  132.0 1.7 pad.17.w_lrem
  133.7 6.9 %reshape_squeeze.23 = bf16[64,4,64,64]{3,2,1,0:T(8,128)(2,1)} reshape(bf16[1,1,4,64,4096]{4,3,2,1,0:T(8,128)(2,1)} %param.11) | data formatting | bytes 4194304 | tf_op jit(solution)/shard_map/reshape;squeeze | solution.py:332
  140.6 12.5 %copy.34 = bf16[64,4,64,64]{3,1,2,0:T(4,128)(2,1)} copy(bf16[64,4,64,64]{3,2,1,0:T(8,128)(2,1)} %reshape_squeeze.23) | data formatting | bytes 4194304 | tf_op jit(solution)/shard_map/reshape;squeeze | solution.py:332
  153.1 0.0 copy-start.1
  153.1 7.1 %reshape.104.w_dinv = bf16[64,64,256]{2,1,0:T(8,128)(2,1)} reshape(bf16[64,64,4,64]{3,2,1,0:T(4,128)(2,1)} %bitcast.56) | data formatting | bytes 4194304 | tf_op jit(solution)/shard_map/reshape | solution.py:334
  160.2 0.0 copy-done.1
  160.2 4.4 %reshape_squeeze.22 = bf16[16,4,3,64,64]{4,3,1,0,2:T(8,128)(2,1)} reshape(bf16[1,1,64,3,4096]{4,2,3,1,0:T(8,128)(2,1)S(1)} %copy-done.1) | data formatting | bytes 3145728 | tf_op jit(solution)/shard_map/reshape;squeeze | solution.py:325
  164.6 4.9 %copy.35 = bf16[16,4,3,64,64]{4,1,3,2,0:T(4,128)(2,1)S(1)} copy(bf16[16,4,3,64,64]{4,3,1,0,2:T(8,128)(2,1)} %reshape_squeeze.22) | data formatting | bytes 3145728 | tf_op jit(solution)/shard_map/reshape;squeeze | solution.py:325
  169.5 3.0 reshape.103
  172.5 0.0 copy-start.2
  172.5 3.0 pad.18.w_urem
  175.6 0.0 copy-done.2
  175.6 1.5 reshape_squeeze.18
  177.1 0.1 copy.36
  177.2 0.0 copy-start.4
  177.3 0.0 copy-start.5
  177.3 2.0 pad_maximum_fusion.rhs
  179.2 0.0 copy-done.4
  179.2 0.1 copy.18
  179.3 0.8 reshape.95.low_idx
  180.1 0.0 copy-done.5
  180.2 0.1 copy.19
  180.3 0.8 reshape.96.up_idx
  181.1 192.7 %sweeps.1 = bf16[4,512,128]{2,1,0:T(8,128)(2,1)} custom-call(s32[576]{0:T(1024)} %reshape.95.low_idx, s32[576]{0:T(1024)} %reshape.96.up_idx, s32[192]{0:T(256)} %copy-done.3, s32[128]{0:T(128)} %copy-done.6, s32[1,1536]{1,0:T(1,128)} %add.57.edge_code, s32[1,1024]{1,0:T(1,128)} %add.61.owner_code, f32[4,64,16,128]{3,2,1,0:T(8,128)} %pad_maximum_fusion.rhs, ...), custom_call_target="tpu_custom_call" | custom-call | tf_op jit(solution)/shard_map/sweeps/pallas_call | solution.py:345
  373.7 2.1 reshape.105
  (2 shorter events, 0.0 us)
Async XLA Ops:
  0.9 16.3 %copy-start.3 = (s32[192]{0:T(256)}, s32[192]{0:T(256)S(1)}, u32[]{:S(2)}) copy-start(s32[192]{0:T(256)S(1)} %reshape.97.slot_idx) | copy-start | bytes 2308
  2.6 14.6 %copy-start.6 = (s32[128]{0:T(128)}, s32[128]{0:T(128)S(1)}, u32[]{:S(2)}) copy-start(s32[128]{0:T(128)S(1)} %reshape.98.send_idx) | copy-start | bytes 1540
  110.3 7.2 %copy-start = (bf16[1,1,64,3,4096]{4,2,3,1,0:T(8,128)(2,1)S(1)}, bf16[1,1,64,3,4096]{4,2,3,1,0:T(8,128)(2,1)}, u32[]{:S(2)}) copy-start(bf16[1,1,64,3,4096]{4,2,3,1,0:T(8,128)(2,1)} %param.16) | copy-start | bytes 4718596
  153.1 7.1 %copy-start.1 = (bf16[1,1,64,3,4096]{4,2,3,1,0:T(8,128)(2,1)S(1)}, bf16[1,1,64,3,4096]{4,2,3,1,0:T(8,128)(2,1)}, u32[]{:S(2)}) copy-start(bf16[1,1,64,3,4096]{4,2,3,1,0:T(8,128)(2,1)} %param.17) | copy-start | bytes 4718596
  172.5 3.0 copy-start.2
  177.2 2.0 copy-start.4
  177.3 2.9 copy-start.5

commit v2 on v1

v2 whole, which is shorter than its diff:
```python
import functools

import jax
import jax.numpy as jnp
from jax import lax
from jax.experimental import pallas as pl
from jax.experimental.pallas import tpu as pltpu
from jax.sharding import PartitionSpec as P

BS = 64
GROUP = 4
MESH = pl.DeviceIdType.MESH
BF16 = jnp.bfloat16
F32 = jnp.float32


def dot_rows(left, right):
    return lax.dot_general(left, right, (((1,), (1,)), ((), ())), preferred_element_type=F32)


def kernel(
    levels,
    parts,
    low_idx,
    up_idx,
    slot_idx,
    send_idx,
    rhs_hbm,
    low_hbm,
    up_hbm,
    lrem_hbm,
    urem_hbm,
    dinv_hbm,
    out,
    raw_rhs,
    raw,
    raw_urem,
    raw_dinv,
    weights,
    w_urem,
    w_dinv,
    rhs,
    mixed,
    solved,
    reduced,
    table,
    rtable,
    boundary,
    upward,
    terms,
    edge_code,
    owner_code,
    edge_hot,
    owner_hot,
    send_f,
    recv_f,
    send_b,
    recv_b,
    sems,
    load_sems,
):
    level = lax.axis_index("level")
    me = lax.axis_index("dom")
    colors, blocks = solved.shape[0], solved.shape[1]
    steps = colors - 1
    groups = blocks // GROUP
    per_peer = send_idx.shape[0]
    rows_per_peer = send_f.shape[0] // parts
    remote_piece = steps
    pieces = 2 * steps + 1

    def piece_source(piece):
        if piece < steps:
            return low_hbm.at[0, 0, piece]
        if piece == steps:
            return lrem_hbm.at[0, 0]
        return up_hbm.at[0, 0, piece - steps - 1]

    load_rhs = pltpu.make_async_copy(rhs_hbm.at[0, 0], raw_rhs, load_sems.at[pieces])
    load_urem = pltpu.make_async_copy(urem_hbm.at[0, 0], raw_urem, load_sems.at[pieces + 1])
    load_dinv = pltpu.make_async_copy(dinv_hbm.at[0, 0], raw_dinv, load_sems.at[pieces + 2])
    load_rhs.start()
    for piece in range(pieces):
        pltpu.make_async_copy(piece_source(piece), raw.at[piece], load_sems.at[piece]).start()
    load_dinv.start()
    load_urem.start()

    barrier = pltpu.get_barrier_semaphore()

    def greet(step, _):
        peer = lax.rem(me + step, parts)

        @pl.when(level > 0)
        def _():
            pl.semaphore_signal(barrier, inc=1, device_id=(level - 1, peer), device_id_type=MESH)

        @pl.when(level < levels - 1)
        def _():
            pl.semaphore_signal(barrier, inc=1, device_id=(level + 1, peer), device_id_type=MESH)

        return 0

    lax.fori_loop(0, parts, greet, 0)

    low_half16 = lax.broadcasted_iota(jnp.int32, (16, 128), 1) < BS
    low_half8 = lax.broadcasted_iota(jnp.int32, (8, 128), 1) < BS
    zero8 = jnp.zeros((8, 128), F32)
    zero16 = jnp.zeros((16, 128), BF16)

    def doubled(packed):
        turned = pltpu.roll(packed, BS, 1)
        return jnp.concatenate(
            [jnp.where(low_half8, packed, turned), jnp.where(low_half8, turned, packed)], axis=0
        )

    def paired(rows):
        return jnp.where(low_half8, rows[:8], rows[8:])

    def interleave(slot, first, second):
        first_turned = pltpu.roll(first, BS, 1)
        second_turned = pltpu.roll(second, BS, 1)
        mixed[slot, pl.ds(0, 8, stride=2), :] = jnp.where(low_half8, first, second_turned)
        mixed[slot, pl.ds(1, 8, stride=2), :] = jnp.where(low_half8, first_turned, second)

    def lines_of(source, first, quarter):
        lanes = slice(quarter * 1024, quarter * 1024 + 1024)
        part = source[pl.ds(pl.multiple_of(first, 16), 16), lanes]
        return part.astype(F32).reshape(16, 8, 128)

    def prepare_piece(piece, _):
        pltpu.make_async_copy(lrem_hbm.at[0, 0], raw.at[piece], load_sems.at[piece]).wait()

        def body(step, _):
            for quarter in range(4):
                lines = [lines_of(raw.at[piece, couple], step * 16, quarter) for couple in range(3)]
                for slot in range(16):
                    interleave(quarter * 32 + slot, lines[0][slot], lines[1][slot])
                    third = lines[2][slot]
                    turned = pltpu.roll(third, BS, 1)
                    at = quarter * 32 + 16 + slot
                    mixed[at, pl.ds(0, 8, stride=2), :] = jnp.where(low_half8, third, zero8)
                    mixed[at, pl.ds(1, 8, stride=2), :] = jnp.where(low_half8, turned, zero8)
                for slot in range(16):
                    group = piece * groups + step * GROUP + slot // GROUP
                    row = (slot % GROUP) * BS + quarter * 16
                    weights[group, row : row + 16, 0:128] = mixed[quarter * 32 + slot].astype(BF16)
                    weights[group, row : row + 16, 128:256] = mixed[quarter * 32 + 16 + slot].astype(BF16)
            return 0

        lax.fori_loop(0, blocks // 16, body, 0)
        return 0

    def prepare_rhs():
        load_rhs.wait()

        def body(step, _):
            color, first = step // (blocks // 8), lax.rem(step, blocks // 8) * 8
            lines = raw_rhs[color, pl.ds(pl.multiple_of(first, 8), 8), :].reshape(8, 8, 128)
            for slot in range(8):
                rhs[color, first + slot] = doubled(lines[slot])
            return 0

        lax.fori_loop(0, colors * blocks // 8, body, 0)

    def prepare_back():
        load_dinv.wait()

        def dinv_body(step, _):
            color, first = step // (blocks // 16), lax.rem(step, blocks // 16) * 16
            for quarter in range(4):
                lines = lines_of(raw_dinv.at[color], first, quarter)
                for pair in range(8):
                    interleave(quarter * 8 + pair, lines[2 * pair], lines[2 * pair + 1])
                for pair in range(8):
                    group = color * groups + first // GROUP + pair // 2
                    lanes = slice((pair % 2) * 128, (pair % 2) * 128 + 128)
                    value = mixed[quarter * 8 + pair].astype(BF16)
                    w_dinv[group, quarter * 16 : quarter * 16 + 16, lanes] = value
            return 0

        lax.fori_loop(0, colors * blocks // 16, dinv_body, 0)
        load_urem.wait()

        def urem_body(step, _):
            for quarter in range(4):
                for couple in range(3):
                    lines = lines_of(raw_urem.at[couple], step * 16, quarter)
                    for pair in range(8):
                        interleave(quarter * 24 + couple * 8 + pair, lines[2 * pair], lines[2 * pair + 1])
                    for pair in range(8):
                        group = step * GROUP + pair // 2
                        lanes = slice((pair % 2) * 128, (pair % 2) * 128 + 128)
                        value = mixed[quarter * 24 + couple * 8 + pair].astype(BF16)
                        row = couple * BS + quarter * 16
                        w_urem[group, row : row + 16, lanes] = value
                        if couple == 2:
                            w_urem[group, row + BS : row + BS + 16, lanes] = value
            return 0

        lax.fori_loop(0, blocks // 16, urem_body, 0)

        lane = lax.broadcasted_iota(jnp.int32, (8, 128), 1)
        for vector in range(edge_code.shape[1] // 128):
            code = jnp.zeros((8, 128), jnp.int32)
            for within in range(16):
                edge = vector * 16 + within
                code = jnp.where(lane // 8 == within, slot_idx[edge % 3, edge // 3] * 8 + lane % 8, code)
            edge_code[:, vector * 128 : vector * 128 + 128] = code
        for vector in range(owner_code.shape[1] // 128):
            code = jnp.zeros((8, 128), jnp.int32)
            for within in range(16):
                slot = vector * 16 + within
                code = jnp.where(
                    lane // 8 == within, send_idx[slot % per_peer, slot // per_peer] * 8 + lane % 8, code
                )
            owner_code[:, vector * 128 : vector * 128 + 128] = code

        def hot(target, codes):
            def body(chunk, _):
                rows = lax.broadcasted_iota(jnp.int32, (64, target.shape[1]), 0) + chunk * 64
                target[pl.ds(pl.multiple_of(chunk * 64, 64), 64), :] = jnp.where(
                    rows == codes[0:1, :], 1.0, 0.0
                ).astype(BF16)
                return 0

            lax.fori_loop(0, target.shape[0] // 64, body, 0)

        hot(edge_hot, edge_code)
        hot(owner_hot, owner_code)

    def product_of(indices, source, piece, group):
        members = []
        for member in range(GROUP):
            first, second, third = [source[at] for at in indices(group * GROUP + member)]
            members.append(jnp.concatenate([jnp.where(low_half16, first, second), third], axis=1))
        return dot_rows(jnp.concatenate(members, axis=0), weights[piece * groups + group])

    def own_block(product, member):
        lanes = slice((member // 2) * 128, (member // 2) * 128 + 128)
        piece = product[member * 16 : member * 16 + 16, lanes]
        turned = pltpu.roll(piece, BS, 1)
        if member % 2 == 0:
            return jnp.where(low_half16, piece, turned)
        return jnp.where(low_half16, turned, piece)

    def spread(source, group):
        members = []
        for member in range(GROUP):
            value = source[group * GROUP + member]
            if member % 2 == 0:
                kept = jnp.where(low_half16, value, zero16)
            else:
                kept = jnp.where(low_half16, zero16, value)
            pair = [kept, zero16] if member < 2 else [zero16, kept]
            members.append(jnp.concatenate(pair, axis=1))
        return jnp.concatenate(members, axis=0)

    def forward_step(piece, indices, source, color):
        def body(group, _):
            product = product_of(indices, source, piece, group)
            for member in range(GROUP):
                block = group * GROUP + member
                solved[color, block] = (rhs[color, block] - own_block(product, member)).astype(BF16)
            return 0

        lax.fori_loop(0, groups, body, 0, unroll=groups)

    def remote_indices(block):
        return [slot_idx[couple, block] for couple in range(3)]

    prepare_rhs()
    ahead = jnp.where(level == 0, 0, jnp.where(level == 1, steps + 1, pieces))
    lax.fori_loop(0, ahead, prepare_piece, 0)

    @pl.when(level >= 2)
    def _():
        prepare_back()

    @pl.when(level == 0)
    def _():
        def body(block, _):
            solved[0, block] = rhs[0, block].astype(BF16)
            return 0

        lax.fori_loop(0, blocks, body, 0, unroll=8)

    @pl.when(level > 0)
    def _():
        pltpu.make_async_copy(recv_f, recv_f, sems.at[1]).wait()

        def body(pair, _):
            both = recv_f[pl.ds(pl.multiple_of(pair * 16, 16), 16), :].astype(F32)
            rtable[pair * 2] = doubled(both[:8]).astype(BF16)
            rtable[pair * 2 + 1] = doubled(both[8:]).astype(BF16)
            return 0

        lax.fori_loop(0, recv_f.shape[0] // 16, body, 0, unroll=8)
        forward_step(remote_piece, remote_indices, rtable, 0)

    def color_body(color, _):
        @pl.when(level == 0)
        def _():
            prepare_piece(color - 1, 0)

        def indices(block):
            return [low_idx[color - 1, couple, block] for couple in range(3)]

        forward_step(color - 1, indices, solved.at[color - 1], color)
        return 0

    lax.fori_loop(1, colors, color_body, 0)

    pl.semaphore_wait(
        barrier, parts * ((level > 0).astype(jnp.int32) + (level < levels - 1).astype(jnp.int32))
    )

    @pl.when(level < levels - 1)
    def _():
        def pack(block, _):
            boundary[block] = paired(solved[colors - 1, block].astype(F32))
            return 0

        lax.fori_loop(0, blocks, pack, 0, unroll=8)

        def push(step, _):
            peer = lax.rem(me + step, parts)
            for pair in range(per_peer // 2):
                both = jnp.concatenate(
                    [boundary[send_idx[pair * 2, peer]], boundary[send_idx[pair * 2 + 1, peer]]], axis=0
                )
                send_f[pl.ds(pl.multiple_of(peer * rows_per_peer + pair * 16, 16), 16), :] = both.astype(BF16)
            pltpu.make_async_remote_copy(
                src_ref=send_f.at[pl.ds(pl.multiple_of(peer * rows_per_peer, 16), rows_per_peer)],
                dst_ref=recv_f.at[pl.ds(pl.multiple_of(me * rows_per_peer, 16), rows_per_peer)],
                send_sem=sems.at[0],
                recv_sem=sems.at[1],
                device_id=(level + 1, peer),
                device_id_type=MESH,
            ).start()
            return 0

        lax.fori_loop(0, parts, push, 0)

    behind = jnp.where(level == 0, steps, jnp.where(level == 1, steps + 1, pieces))
    lax.fori_loop(behind, pieces, prepare_piece, 0)

    @pl.when(level < 2)
    def _():
        prepare_back()

    def finish(color):
        def body(group, _):
            inverses = w_dinv[color * groups + group]
            product = dot_rows(spread(reduced, group), jnp.concatenate([inverses, inverses], axis=0))
            results = []
            for member in range(GROUP):
                value = product[member * 16 : member * 16 + 16]
                table[color, group * GROUP + member] = value.astype(BF16)
                results.append(paired(value))
            at = pl.ds(pl.multiple_of(group * GROUP * 8, GROUP * 8), GROUP * 8)
            out[color, at, :] = jnp.concatenate(results, axis=0).astype(BF16)
            return 0

        lax.fori_loop(0, groups, body, 0, unroll=groups)

    @pl.when(level == levels - 1)
    def _():
        upward[...] = jnp.zeros_like(upward)

    @pl.when(level < levels - 1)
    def _():
        pltpu.make_async_copy(recv_b, recv_b, sems.at[3]).wait()
        upward[...] = jnp.dot(owner_hot[...], recv_b[...], preferred_element_type=F32)

    def last_color(block, _):
        add = doubled(upward[pl.ds(pl.multiple_of(block * 8, 8), 8), :])
        reduced[block] = (solved[colors - 1, block].astype(F32) - add).astype(BF16)
        return 0

    lax.fori_loop(0, blocks, last_color, 0, unroll=16)

    def back_color(step, _):
        color = colors - 2 - step
        finish(color + 1)
        source = table.at[color + 1]

        def indices(block):
            return [up_idx[color, couple, block] for couple in range(3)]

        def body(group, _):
            product = product_of(indices, source, steps + 1 + color, group)
            for member in range(GROUP):
                block = group * GROUP + member
                value = solved[color, block].astype(F32) - own_block(product, member)
                reduced[block] = value.astype(BF16)
            return 0

        lax.fori_loop(0, groups, body, 0, unroll=groups)
        return 0

    lax.fori_loop(0, steps, back_color, 0)
    finish(0)

    @pl.when(level > 0)
    def _():
        def body(group, _):
            product = dot_rows(spread(table.at[0], group), w_urem[group])
            results = []
            for member in range(GROUP):
                rows = product[member * 16 : member * 16 + 16]
                both, third = rows[:, :128], rows[:, 128:]
                turned = pltpu.roll(both, BS, 1)
                results.append(jnp.where(low_half8, both[:8], turned[8:]))
                results.append(jnp.where(low_half8, turned[:8], both[8:]))
                results.append(paired(third))
            at = pl.ds(pl.multiple_of(group * GROUP * 24, 96), GROUP * 24)
            terms[at, :] = jnp.concatenate(results, axis=0).astype(BF16)
            return 0

        lax.fori_loop(0, groups, body, 0, unroll=groups)
        send_b[...] = jnp.dot(edge_hot[...], terms[...], preferred_element_type=F32).astype(BF16)

        def push(step, _):
            peer = lax.rem(me + step, parts)
            pltpu.make_async_remote_copy(
                src_ref=send_b.at[pl.ds(pl.multiple_of(peer * rows_per_peer, 16), rows_per_peer)],
                dst_ref=recv_b.at[pl.ds(pl.multiple_of(me * rows_per_peer, 16), rows_per_peer)],
                send_sem=sems.at[2],
                recv_sem=sems.at[3],
                device_id=(level - 1, peer),
                device_id_type=MESH,
            ).start()
            return 0

        lax.fori_loop(0, parts, push, 0)
        pltpu.make_async_copy(send_b, send_b, sems.at[2]).wait()

    @pl.when(level < levels - 1)
    def _():
        pltpu.make_async_copy(send_f, send_f, sems.at[0]).wait()


def per_device(
    levels,
    parts,
    rhs,
    dinv,
    lower_local,
    lower_nbrs,
    upper_local,
    upper_nbrs,
    lower_remote,
    upper_remote,
    remote_slots,
    send_list,
):
    colors, blocks, features = rhs.shape[2:]
    entries = dinv.shape[-1]
    steps, pieces = colors - 1, 2 * colors - 1
    groups = blocks // GROUP
    slots = parts * send_list.shape[-1]

    smem = pl.BlockSpec(memory_space=pltpu.SMEM)
    vmem = pl.BlockSpec(memory_space=pltpu.VMEM)
    hbm = pl.BlockSpec(memory_space=pl.ANY)
    answer = pl.pallas_call(
        functools.partial(kernel, levels, parts),
        out_shape=jax.ShapeDtypeStruct((colors, blocks * 8, 128), BF16),
        in_specs=[smem] * 4 + [hbm] * 6,
        out_specs=vmem,
        scratch_shapes=[
            pltpu.VMEM((colors, blocks, features), F32),
            pltpu.VMEM((pieces, 3, blocks, entries), BF16),
            pltpu.VMEM((3, blocks, entries), BF16),
            pltpu.VMEM((colors, blocks, entries), BF16),
            pltpu.VMEM((pieces * groups, GROUP * BS, 256), BF16),
            pltpu.VMEM((groups, 256, GROUP * BS), BF16),
            pltpu.VMEM((colors * groups, BS, GROUP * BS), BF16),
            pltpu.VMEM((colors, blocks, 16, 128), F32),
            pltpu.VMEM((128, 16, 128), F32),
            pltpu.VMEM((colors, blocks, 16, 128), BF16),
            pltpu.VMEM((blocks, 16, 128), BF16),
            pltpu.VMEM((colors, blocks, 16, 128), BF16),
            pltpu.VMEM((slots, 16, 128), BF16),
            pltpu.VMEM((blocks, 8, 128), F32),
            pltpu.VMEM((blocks * 8, 128), F32),
            pltpu.VMEM((blocks * 24, 128), BF16),
            pltpu.VMEM((8, blocks * 24), jnp.int32),
            pltpu.VMEM((8, slots * 8), jnp.int32),
            pltpu.VMEM((slots * 8, blocks * 24), BF16),
            pltpu.VMEM((blocks * 8, slots * 8), BF16),
            pltpu.VMEM((slots * 8, 128), BF16),
            pltpu.VMEM((slots * 8, 128), BF16),
            pltpu.VMEM((slots * 8, 128), BF16),
            pltpu.VMEM((slots * 8, 128), BF16),
            pltpu.SemaphoreType.DMA((4,)),
            pltpu.SemaphoreType.DMA((pieces + 3,)),
        ],
        compiler_params=pltpu.CompilerParams(
            collective_id=0, has_side_effects=True, vmem_limit_bytes=60 * 1024 * 1024
        ),
        name="sweeps",
    )(
        jnp.swapaxes(lower_nbrs[0, 0], 1, 2),
        jnp.swapaxes(upper_nbrs[0, 0], 1, 2),
        jnp.swapaxes(remote_slots[0, 0], 0, 1),
        jnp.swapaxes(send_list[0, 0], 0, 1),
        rhs,
        jnp.swapaxes(lower_local, 3, 4),
        jnp.swapaxes(upper_local, 3, 4),
        jnp.swapaxes(lower_remote, 2, 3),
        jnp.swapaxes(upper_remote, 2, 3),
        dinv,
    )
    return answer.reshape(1, 1, colors, blocks, features)


def solution(mesh):
    levels, parts = mesh.shape["level"], mesh.shape["dom"]
    return jax.shard_map(
        functools.partial(per_device, levels, parts),
        mesh=mesh,
        in_specs=(
            P("level", "dom", None, None, None),
            P("level", "dom", None, None, None),
            P("level", "dom", None, None, None, None),
            P("level", "dom", None, None, None),
            P("level", "dom", None, None, None, None),
            P("level", "dom", None, None, None),
            P("level", "dom", None, None, None),
            P("level", "dom", None, None, None),
            P("level", "dom", None, None),
            P("level", "dom", None, None),
        ),
        out_specs=P("level", "dom", None, None, None),
        check_vma=False,
    )
```

time: 379 us -> 142 us (0.37)
  local copies, waits for them, and re-layouts: 181 us -> 4.62 us
  Pallas kernels: 193 us -> 137 us
    another operation x12 -> x0, local copies, waits for them, and re-layouts: 93.8 us -> none  [the longest x6 63.4 us: coupling_rows(): split = matrices.reshape(count, blocks, 3, BS, BS).transpose(0, 1, 3, 2, 4)]
    reshape x12 -> x0, local copies, waits for them, and re-layouts: 62.8 us -> none  [the longest x6 50.8 us: coupling_rows(): flat = split.reshape(count * groups, GROUP * BS, 3 * BS)]
    pallas_call x1, Pallas kernels: 193 us -> 137 us  [per_device(): pl.pallas_call(functools.partial(kernel, levels, parts), out_shape=jax.Sh...]
    pad x4 -> x0, local copies, waits for them, and re-layouts: 19 us -> none  [the longest x3 16 us: coupling_rows(): return jnp.pad(flat, ((0, 0), (0, 0), (0, BS)))]
where the time goes in v2:
time: 142 us; the launch traced here: 141 us
  Pallas kernels  137 us (96%)
  local copies, waits for them, and re-layouts  4.62 us (3%)
    pallas_call x1, Pallas kernels, per_device(): pl.pallas_call(functools.partial(kernel, levels, parts), out_shape=jax.Sh...  137 us

profile of v2, /device:TPU:1, one launch (start us, length us, event | category | flops | bytes accessed | tf_op | source)
XLA Modules:
  0.0 141.3 jit_solution(17122030688207460558)
XLA Ops:
  0.0 1.3 copy.17
  1.3 1.3 copy_bitcast_fusion
  2.6 136.7 %sweeps.1 = bf16[4,512,128]{2,1,0:T(8,128)(2,1)} custom-call(s32[3,3,64]{2,1,0:T(4,128)} %get-tuple-element.6.low_idx, s32[3,3,64]{2,1,0:T(4,128)} %get-tuple-element.5.up_idx, s32[3,64]{1,0:T(4,128)} %bitcast.24, s32[4,32]{1,0:T(4,128)} %bitcast.25, f32[1,1,4,64,1024]{4,3,2,1,0:T(8,128)} %rhs_hbm.1, bf16[1,1,3,3,64,4096]{5,4,3,2,1,0:T(8,128)(2,1)} %bitcast.20, ...), custom_call_target="tpu_custom_call" | custom-call | tf_op jit(solution)/shard_map/sweeps/pallas_call | solution.py:466
  139.3 2.1 %reshape.3 = bf16[1,1,4,64,1024]{4,3,2,1,0:T(8,128)(2,1)} reshape(bf16[4,512,128]{2,1,0:T(8,128)(2,1)} %sweeps.1) | data formatting | bytes 1048576 | tf_op jit(solution)/shard_map/reshape | solution.py:515

commit v3 on v2

--- a/solution.py
+++ b/solution.py
@@ -260,10 +260,11 @@
             product = product_of(indices, source, piece, group)
             for member in range(GROUP):
                 block = group * GROUP + member
-                solved[color, block] = (rhs[color, block] - own_block(product, member)).astype(BF16)
+                reduced[block] = (rhs[color, block] - own_block(product, member)).astype(BF16)
             return 0
 
         lax.fori_loop(0, groups, body, 0, unroll=groups)
+        solved[color] = reduced[...]
 
     def remote_indices(block):
         return [slot_idx[couple, block] for couple in range(3)]

time: 142 us -> 113 us (0.80)
  Pallas kernels: 137 us -> 108 us
    pallas_call x1, Pallas kernels: 137 us -> 108 us  [per_device(): pl.pallas_call(functools.partial(kernel, levels, parts), out_shape=jax.Sh...]
where the time goes in v3:
time: 113 us; the launch traced here: 112 us
  Pallas kernels  108 us (96%)
  local copies, waits for them, and re-layouts  4.62 us (4%)
    pallas_call x1, Pallas kernels, per_device(): pl.pallas_call(functools.partial(kernel, levels, parts), out_shape=jax.Sh...  108 us

profile of v3, /device:TPU:1, one launch (start us, length us, event | category | flops | bytes accessed | tf_op | source)
XLA Modules:
  0.0 112.4 jit_solution(3317863729847455206)
XLA Ops:
  0.0 1.3 %copy.17 = s32[1,1,64,3]{2,3,1,0:T(4,128)} copy(s32[1,1,64,3]{2,1,3,0:T(1,128)} %param.18) | data formatting | bytes 1536
  1.3 1.3 %copy_bitcast_fusion = (s32[3,3,64]{2,1,0:T(4,128)}, s32[3,3,64]{2,1,0:T(4,128)}) fusion(s32[1,1,3,64,3]{3,1,4,2,0:T(1,128)} %param.15, s32[1,1,3,64,3]{3,1,4,2,0:T(1,128)} %param.13), kind=kLoop, calls=%fused_computation | loop fusion | bytes 9216 | tf_op jit(solution)/shard_map/transpose | solution.py:506
  2.6 107.8 %sweeps.1 = bf16[4,512,128]{2,1,0:T(8,128)(2,1)} custom-call(s32[3,3,64]{2,1,0:T(4,128)} %get-tuple-element.6.low_idx, s32[3,3,64]{2,1,0:T(4,128)} %get-tuple-element.5.up_idx, s32[3,64]{1,0:T(4,128)} %bitcast.24, s32[4,32]{1,0:T(4,128)} %bitcast.25, f32[1,1,4,64,1024]{4,3,2,1,0:T(8,128)} %rhs_hbm.1, bf16[1,1,3,3,64,4096]{5,4,3,2,1,0:T(8,128)(2,1)} %bitcast.20, ...), custom_call_target="tpu_custom_call" | custom-call | tf_op jit(solution)/shard_map/sweeps/pallas_call | solution.py:467
  110.3 2.1 %reshape.3 = bf16[1,1,4,64,1024]{4,3,2,1,0:T(8,128)(2,1)} reshape(bf16[4,512,128]{2,1,0:T(8,128)(2,1)} %sweeps.1) | data formatting | bytes 1048576 | tf_op jit(solution)/shard_map/reshape | solution.py:516

commit v4 on v3

--- a/solution.py
+++ b/solution.py
@@ -16,6 +16,15 @@
 
 def dot_rows(left, right):
     return lax.dot_general(left, right, (((1,), (1,)), ((), ())), preferred_element_type=F32)
+
+
+def far_first(parts):
+    if parts != 32:
+        return [(0, 0, step) for step in range(parts)], (1, 1, parts)
+    hops = lambda step: min(step, 4 - step)
+    steps = [(z, y, core) for z in range(4) for y in range(4) for core in range(2)]
+    steps.sort(key=lambda at: -(hops(at[0]) + hops(at[1]) + 0.5 * at[2]))
+    return steps, (4, 4, 2)
 
 
 def kernel(
@@ -36,13 +45,17 @@
     raw,
     raw_urem,
     raw_dinv,
-    weights,
-    w_urem,
+    flat,
+    mats,
+    mat_urem,
     w_dinv,
+    mat_dinv,
+    identity,
     rhs,
     mixed,
     solved,
     reduced,
+    base,
     table,
     rtable,
     boundary,
@@ -66,6 +79,13 @@
     groups = blocks // GROUP
     per_peer = send_idx.shape[0]
     rows_per_peer = send_f.shape[0] // parts
+    offsets, sides = far_first(parts)
+    at_z, at_y, at_core = me // (sides[1] * sides[2]), lax.rem(me // sides[2], sides[1]), lax.rem(me, sides[2])
+    peers = [
+        (lax.rem(at_z + z, sides[0]) * sides[1] + lax.rem(at_y + y, sides[1])) * sides[2]
+        + lax.rem(at_core + core, sides[2])
+        for z, y, core in offsets
+    ]
     remote_piece = steps
     pieces = 2 * steps + 1
 
@@ -80,10 +100,12 @@
     load_urem = pltpu.make_async_copy(urem_hbm.at[0, 0], raw_urem, load_sems.at[pieces + 1])
     load_dinv = pltpu.make_async_copy(dinv_hbm.at[0, 0], raw_dinv, load_sems.at[pieces + 2])
     load_rhs.start()
-    for piece in range(pieces):
+    for piece in range(steps + 1):
         pltpu.make_async_copy(piece_source(piece), raw.at[piece], load_sems.at[piece]).start()
     load_dinv.start()
     load_urem.start()
+    for piece in range(steps + 1, pieces):
+        pltpu.make_async_copy(piece_source(piece), raw.at[piece], load_sems.at[piece]).start()
 
     barrier = pltpu.get_barrier_semaphore()
 
@@ -127,8 +149,11 @@
         part = source[pl.ds(pl.multiple_of(first, 16), 16), lanes]
         return part.astype(F32).reshape(16, 8, 128)
 
-    def prepare_piece(piece, _):
+    def await_piece(piece):
         pltpu.make_async_copy(lrem_hbm.at[0, 0], raw.at[piece], load_sems.at[piece]).wait()
+
+    def flatten_piece(piece):
+        await_piece(piece)
 
         def body(step, _):
             for quarter in range(4):
@@ -141,13 +166,44 @@
                     mixed[at, pl.ds(0, 8, stride=2), :] = jnp.where(low_half8, third, zero8)
                     mixed[at, pl.ds(1, 8, stride=2), :] = jnp.where(low_half8, turned, zero8)
                 for slot in range(16):
-                    group = piece * groups + step * GROUP + slot // GROUP
+                    group = step * GROUP + slot // GROUP
                     row = (slot % GROUP) * BS + quarter * 16
-                    weights[group, row : row + 16, 0:128] = mixed[quarter * 32 + slot].astype(BF16)
-                    weights[group, row : row + 16, 128:256] = mixed[quarter * 32 + 16 + slot].astype(BF16)
+                    flat[group, row : row + 16, 0:128] = mixed[quarter * 32 + slot].astype(BF16)
+                    flat[group, row : row + 16, 128:256] = mixed[quarter * 32 + 16 + slot].astype(BF16)
             return 0
 
         lax.fori_loop(0, blocks // 16, body, 0)
+
+    def turned(rows):
+        return dot_rows(identity[...], rows).astype(BF16)
+
+    def prepare_lower(piece, _):
+        flatten_piece(piece)
+
+        def body(group, _):
+            mats[piece * groups + group] = turned(flat[group])
+            return 0
+
+        lax.fori_loop(0, groups, body, 0, unroll=4)
+        return 0
+
+    member_lane = lax.broadcasted_iota(jnp.int32, (BS, GROUP * BS), 1) // BS
+
+    def prepare_upper(color, _):
+        piece = steps + 1 + color
+        flatten_piece(piece)
+
+        def body(group, _):
+            inverses = w_dinv[color * groups + group]
+            apart = [
+                jnp.where(member_lane == member, inverses, jnp.zeros_like(inverses))
+                for member in range(GROUP)
+            ]
+            product = dot_rows(turned(flat[group]), jnp.concatenate(apart, axis=0))
+            mats[piece * groups + group] = product.astype(BF16)
+            return 0
+
+        lax.fori_loop(0, groups, body, 0, unroll=4)
         return 0
 
     def prepare_rhs():
@@ -160,9 +216,9 @@
                 rhs[color, first + slot] = doubled(lines[slot])
             return 0
 
-        lax.fori_loop(0, colors * blocks // 8, body, 0)
-
-    def prepare_back():
+        lax.fori_loop(0, colors * blocks // 8, body, 0, unroll=2)
+
+    def prepare_sums():
         load_dinv.wait()
 
         def dinv_body(step, _):
@@ -179,6 +235,13 @@
             return 0
 
         lax.fori_loop(0, colors * blocks // 16, dinv_body, 0)
+
+        def dinv_turn(group, _):
+            inverses = w_dinv[group]
+            mat_dinv[group] = turned(jnp.concatenate([inverses, inverses], axis=0))
+            return 0
+
+        lax.fori_loop(0, colors * groups, dinv_turn, 0, unroll=4)
         load_urem.wait()
 
         def urem_body(step, _):
@@ -192,19 +255,25 @@
                         lanes = slice((pair % 2) * 128, (pair % 2) * 128 + 128)
                         value = mixed[quarter * 24 + couple * 8 + pair].astype(BF16)
                         row = couple * BS + quarter * 16
-                        w_urem[group, row : row + 16, lanes] = value
+                        flat[group, row : row + 16, lanes] = value
                         if couple == 2:
-                            w_urem[group, row + BS : row + BS + 16, lanes] = value
+                            flat[group, row + BS : row + BS + 16, lanes] = value
             return 0
 
         lax.fori_loop(0, blocks // 16, urem_body, 0)
+
+        def urem_turn(group, _):
+            mat_urem[group] = turned(flat[group])
+            return 0
+
+        lax.fori_loop(0, groups, urem_turn, 0, unroll=4)
 
         lane = lax.broadcasted_iota(jnp.int32, (8, 128), 1)
         for vector in range(edge_code.shape[1] // 128):
             code = jnp.zeros((8, 128), jnp.int32)
             for within in range(16):
                 edge = vector * 16 + within
-                code = jnp.where(lane // 8 == within, slot_idx[edge % 3, edge // 3] * 8 + lane % 8, code)
+                code = jnp.where(lane // 8 == within, slot_idx[0, edge % 3, 0, edge // 3] * 8 + lane % 8, code)
             edge_code[:, vector * 128 : vector * 128 + 128] = code
         for vector in range(owner_code.shape[1] // 128):
             code = jnp.zeros((8, 128), jnp.int32)
@@ -228,12 +297,12 @@
         hot(edge_hot, edge_code)
         hot(owner_hot, owner_code)
 
-    def product_of(indices, source, piece, group):
+    def gathered(indices, source, group):
         members = []
         for member in range(GROUP):
             first, second, third = [source[at] for at in indices(group * GROUP + member)]
             members.append(jnp.concatenate([jnp.where(low_half16, first, second), third], axis=1))
-        return dot_rows(jnp.concatenate(members, axis=0), weights[piece * groups + group])
+        return jnp.concatenate(members, axis=0)
 
     def own_block(product, member):
         lanes = slice((member // 2) * 128, (member // 2) * 128 + 128)
@@ -255,9 +324,9 @@
             members.append(jnp.concatenate(pair, axis=1))
         return jnp.concatenate(members, axis=0)
 
-    def forward_step(piece, indices, source, color):
+    def forward_step(multiply, indices, source, color):
         def body(group, _):
-            product = product_of(indices, source, piece, group)
+            product = multiply(gathered(indices, source, group), group)
             for member in range(GROUP):
                 block = group * GROUP + member
                 reduced[block] = (rhs[color, block] - own_block(product, member)).astype(BF16)
@@ -266,16 +335,18 @@
         lax.fori_loop(0, groups, body, 0, unroll=groups)
         solved[color] = reduced[...]
 
+    def by_piece(piece):
+        return lambda rows, group: jnp.dot(
+            rows, mats[piece * groups + group], preferred_element_type=F32
+        )
+
     def remote_indices(block):
-        return [slot_idx[couple, block] for couple in range(3)]
+        return [slot_idx[0, couple, 0, block] for couple in range(3)]
+
+    def lower_indices(color):
+        return lambda block: [low_idx[0, color - 1, couple, 0, block] for couple in range(3)]
 
     prepare_rhs()
-    ahead = jnp.where(level == 0, 0, jnp.where(level == 1, steps + 1, pieces))
-    lax.fori_loop(0, ahead, prepare_piece, 0)
-
-    @pl.when(level >= 2)
-    def _():
-        prepare_back()
 
     @pl.when(level == 0)
     def _():
@@ -284,6 +355,34 @@
             return 0
 
         lax.fori_loop(0, blocks, body, 0, unroll=8)
+
+        def color_body(color, _):
+            flatten_piece(color - 1)
+            forward_step(
+                lambda rows, group: dot_rows(rows, flat[group]),
+                lower_indices(color),
+                solved.at[color - 1],
+                color,
+            )
+            return 0
+
+        lax.fori_loop(1, colors, color_body, 0)
+
+    identity[...] = jnp.where(
+        lax.broadcasted_iota(jnp.int32, (256, 256), 0) == lax.broadcasted_iota(jnp.int32, (256, 256), 1),
+        1.0,
+        0.0,
+    ).astype(BF16)
+
+    @pl.when(level > 0)
+    def _():
+        lax.fori_loop(0, steps + 1, prepare_lower, 0)
+
+    @pl.when(level >= 2)
+    def _():
+        prepare_sums()
+
+    lax.fori_loop(0, jnp.where(level == levels - 1, steps, 0), prepare_upper, 0)
 
     @pl.when(level > 0)
     def _():
@@ -296,20 +395,13 @@
             return 0
 
         lax.fori_loop(0, recv_f.shape[0] // 16, body, 0, unroll=8)
-        forward_step(remote_piece, remote_indices, rtable, 0)
-
-    def color_body(color, _):
-        @pl.when(level == 0)
-        def _():
-            prepare_piece(color - 1, 0)
-
-        def indices(block):
-            return [low_idx[color - 1, couple, block] for couple in range(3)]
-
-        forward_step(color - 1, indices, solved.at[color - 1], color)
-        return 0
-
-    lax.fori_loop(1, colors, color_body, 0)
+        forward_step(by_piece(remote_piece), remote_indices, rtable, 0)
+
+        def color_body(color, _):
+            forward_step(by_piece(color - 1), lower_indices(color), solved.at[color - 1], color)
+            return 0
+
+        lax.fori_loop(1, colors, color_body, 0)
 
     pl.semaphore_wait(
         barrier, parts * ((level > 0).astype(jnp.int32) + (level < levels - 1).astype(jnp.int32))
@@ -323,8 +415,7 @@
 
         lax.fori_loop(0, blocks, pack, 0, unroll=8)
 
-        def push(step, _):
-            peer = lax.rem(me + step, parts)
+        for peer in peers:
             for pair in range(per_peer // 2):
                 both = jnp.concatenate(
                     [boundary[send_idx[pair * 2, peer]], boundary[send_idx[pair * 2 + 1, peer]]], axis=0
@@ -338,31 +429,45 @@
                 device_id=(level + 1, peer),
                 device_id_type=MESH,
             ).start()
-            return 0
-
-        lax.fori_loop(0, parts, push, 0)
-
-    behind = jnp.where(level == 0, steps, jnp.where(level == 1, steps + 1, pieces))
-    lax.fori_loop(behind, pieces, prepare_piece, 0)
+
+    @pl.when(level == 0)
+    def _():
+        await_piece(remote_piece)
 
     @pl.when(level < 2)
     def _():
-        prepare_back()
-
-    def finish(color):
+        prepare_sums()
+
+    lax.fori_loop(0, jnp.where(level == levels - 1, 0, steps), prepare_upper, 0)
+
+    def scale(color, source, put):
         def body(group, _):
-            inverses = w_dinv[color * groups + group]
-            product = dot_rows(spread(reduced, group), jnp.concatenate([inverses, inverses], axis=0))
-            results = []
+            product = jnp.dot(
+                spread(source, group), mat_dinv[color * groups + group], preferred_element_type=F32
+            )
             for member in range(GROUP):
-                value = product[member * 16 : member * 16 + 16]
-                table[color, group * GROUP + member] = value.astype(BF16)
-                results.append(paired(value))
+                put(group * GROUP + member, product[member * 16 : member * 16 + 16])
+            return 0
+
+        lax.fori_loop(0, groups, body, 0, unroll=groups)
+
+    def scale_solved(color, _):
+        def put(block, value):
+            base[color, block] = value
+
+        scale(color, solved.at[color], put)
+        return 0
+
+    lax.fori_loop(0, steps, scale_solved, 0)
+
+    def store_out(color):
+        def body(group, _):
+            values = [paired(table[color, group * GROUP + member].astype(F32)) for member in range(GROUP)]
             at = pl.ds(pl.multiple_of(group * GROUP * 8, GROUP * 8), GROUP * 8)
-            out[color, at, :] = jnp.concatenate(results, axis=0).astype(BF16)
-            return 0
-
-        lax.fori_loop(0, groups, body, 0, unroll=groups)
+            out[color, at, :] = jnp.concatenate(values, axis=0).astype(BF16)
+            return 0
+
+        lax.fori_loop(0, groups, body, 0, unroll=4)
 
     @pl.when(level == levels - 1)
     def _():
@@ -380,32 +485,38 @@
 
     lax.fori_loop(0, blocks, last_color, 0, unroll=16)
 
+    def put_last(block, value):
+        table[colors - 1, block] = value.astype(BF16)
+
+    scale(colors - 1, reduced, put_last)
+
     def back_color(step, _):
         color = colors - 2 - step
-        finish(color + 1)
         source = table.at[color + 1]
+        multiply = by_piece(steps + 1 + color)
 
         def indices(block):
-            return [up_idx[color, couple, block] for couple in range(3)]
+            return [up_idx[0, color, couple, 0, block] for couple in range(3)]
 
         def body(group, _):
-            product = product_of(indices, source, steps + 1 + color, group)
+            product = multiply(gathered(indices, source, group), group)
             for member in range(GROUP):
                 block = group * GROUP + member
-                value = solved[color, block].astype(F32) - own_block(product, member)
-                reduced[block] = value.astype(BF16)
+                reduced[block] = (base[color, block] - own_block(product, member)).astype(BF16)
             return 0
 
         lax.fori_loop(0, groups, body, 0, unroll=groups)
+        table[color] = reduced[...]
         return 0
 
     lax.fori_loop(0, steps, back_color, 0)
-    finish(0)
 
     @pl.when(level > 0)
     def _():
         def body(group, _):
-            product = dot_rows(spread(table.at[0], group), w_urem[group])
+            product = jnp.dot(
+                spread(table.at[0], group), mat_urem[group], preferred_element_type=F32
+            )
             results = []
             for member in range(GROUP):
                 rows = product[member * 16 : member * 16 + 16]
@@ -421,8 +532,7 @@
         lax.fori_loop(0, groups, body, 0, unroll=groups)
         send_b[...] = jnp.dot(edge_hot[...], terms[...], preferred_element_type=F32).astype(BF16)
 
-        def push(step, _):
-            peer = lax.rem(me + step, parts)
+        for peer in peers:
             pltpu.make_async_remote_copy(
                 src_ref=send_b.at[pl.ds(pl.multiple_of(peer * rows_per_peer, 16), rows_per_peer)],
                 dst_ref=recv_b.at[pl.ds(pl.multiple_of(me * rows_per_peer, 16), rows_per_peer)],
@@ -431,9 +541,15 @@
                 device_id=(level - 1, peer),
                 device_id_type=MESH,
             ).start()
-            return 0
-
-        lax.fori_loop(0, parts, push, 0)
+
+    def color_out(color, _):
+        store_out(color)
+        return 0
+
+    lax.fori_loop(0, colors, color_out, 0)
+
+    @pl.when(level > 0)
+    def _():
         pltpu.make_async_copy(send_b, send_b, sems.at[2]).wait()
 
     @pl.when(level < levels - 1)
@@ -474,13 +590,17 @@
             pltpu.VMEM((pieces, 3, blocks, entries), BF16),
             pltpu.VMEM((3, blocks, entries), BF16),
             pltpu.VMEM((colors, blocks, entries), BF16),
-            pltpu.VMEM((pieces * groups, GROUP * BS, 256), BF16),
-            pltpu.VMEM((groups, 256, GROUP * BS), BF16),
+            pltpu.VMEM((groups, GROUP * BS, 256), BF16),
+            pltpu.VMEM((pieces * groups, 256, GROUP * BS), BF16),
+            pltpu.VMEM((groups, GROUP * BS, 256), BF16),
             pltpu.VMEM((colors * groups, BS, GROUP * BS), BF16),
+            pltpu.VMEM((colors * groups, GROUP * BS, 2 * BS), BF16),
+            pltpu.VMEM((256, 256), BF16),
             pltpu.VMEM((colors, blocks, 16, 128), F32),
             pltpu.VMEM((128, 16, 128), F32),
             pltpu.VMEM((colors, blocks, 16, 128), BF16),
             pltpu.VMEM((blocks, 16, 128), BF16),
+            pltpu.VMEM((steps, blocks, 16, 128), F32),
             pltpu.VMEM((colors, blocks, 16, 128), BF16),
             pltpu.VMEM((slots, 16, 128), BF16),
             pltpu.VMEM((blocks, 8, 128), F32),
@@ -502,9 +622,9 @@
         ),
         name="sweeps",
     )(
-        jnp.swapaxes(lower_nbrs[0, 0], 1, 2),
-        jnp.swapaxes(upper_nbrs[0, 0], 1, 2),
-        jnp.swapaxes(remote_slots[0, 0], 0, 1),
+        jnp.transpose(lower_nbrs, (0, 2, 4, 1, 3)),
+        jnp.transpose(upper_nbrs, (0, 2, 4, 1, 3)),
+        jnp.transpose(remote_slots, (0, 3, 1, 2)),
         jnp.swapaxes(send_list[0, 0], 0, 1),
         rhs,
         jnp.swapaxes(lower_local, 3, 4),

time: 113 us -> 92.7 us (0.82)
  Pallas kernels: 108 us -> 90.4 us
  local copies, waits for them, and re-layouts: 4.62 us -> 2.06 us
    pallas_call x1, Pallas kernels: 108 us -> 90.4 us  [per_device(): pl.pallas_call(functools.partial(kernel, levels, parts), out_shape=jax.Sh...]
    transpose x1 -> x0, local copies, waits for them, and re-layouts: 1.3 us -> none  [per_device(): jnp.swapaxes(upper_nbrs[0, 0], 1, 2)]
    unnamed x1 -> x0, local copies, waits for them, and re-layouts: 1.26 us -> none
where the time goes in v4:
time: 92.7 us; the launch traced here: 92.5 us
  Pallas kernels  90.4 us (98%)
  local copies, waits for them, and re-layouts  2.06 us (2%)
    pallas_call x1, Pallas kernels, per_device(): pl.pallas_call(functools.partial(kernel, levels, parts), out_shape=jax.Sh...  90.4 us
    reshape x1, local copies, waits for them, and re-layouts, per_device(): return answer.reshape(1, 1, colors, blocks, features)  2.06 us

profile of v4, /device:TPU:1, one launch (start us, length us, event | category | flops | bytes accessed | tf_op | source)
XLA Modules:
  0.0 92.5 jit_solution(10799075198094047999)
XLA Ops:
  0.0 90.4 %sweeps.1 = bf16[4,512,128]{2,1,0:T(8,128)(2,1)} custom-call(s32[1,3,3,1,64]{4,3,2,1,0:T(1,128)} %bitcast.14, s32[1,3,3,1,64]{4,3,2,1,0:T(1,128)} %bitcast.15, s32[1,3,1,64]{3,2,1,0:T(1,128)} %bitcast.17, s32[4,32]{1,0:T(4,128)} %bitcast.16, f32[1,1,4,64,1024]{4,3,2,1,0:T(8,128)} %rhs_hbm.1, bf16[1,1,3,3,64,4096]{5,4,3,2,1,0:T(8,128)(2,1)} %bitcast.10, ...), custom_call_target="tpu_custom_call" | custom-call | tf_op jit(solution)/shard_map/sweeps/pallas_call | solution.py:583
  90.4 2.1 %reshape.3 = bf16[1,1,4,64,1024]{4,3,2,1,0:T(8,128)(2,1)} reshape(bf16[4,512,128]{2,1,0:T(8,128)(2,1)} %sweeps.1) | data formatting | bytes 1048576 | tf_op jit(solution)/shard_map/reshape | solution.py:636

commit v5 on v4

--- a/solution.py
+++ b/solution.py
@@ -9,6 +9,7 @@
 
 BS = 64
 GROUP = 4
+DEPTH = 3 * BS
 MESH = pl.DeviceIdType.MESH
 BF16 = jnp.bfloat16
 F32 = jnp.float32
@@ -126,7 +127,6 @@
 
     low_half16 = lax.broadcasted_iota(jnp.int32, (16, 128), 1) < BS
     low_half8 = lax.broadcasted_iota(jnp.int32, (8, 128), 1) < BS
-    zero8 = jnp.zeros((8, 128), F32)
     zero16 = jnp.zeros((16, 128), BF16)
 
     def doubled(packed):
@@ -163,25 +163,27 @@
                     third = lines[2][slot]
                     turned = pltpu.roll(third, BS, 1)
                     at = quarter * 32 + 16 + slot
-                    mixed[at, pl.ds(0, 8, stride=2), :] = jnp.where(low_half8, third, zero8)
-                    mixed[at, pl.ds(1, 8, stride=2), :] = jnp.where(low_half8, turned, zero8)
+                    mixed[at, pl.ds(0, 8, stride=2), :] = third
+                    mixed[at, pl.ds(1, 8, stride=2), :] = turned
                 for slot in range(16):
                     group = step * GROUP + slot // GROUP
                     row = (slot % GROUP) * BS + quarter * 16
                     flat[group, row : row + 16, 0:128] = mixed[quarter * 32 + slot].astype(BF16)
-                    flat[group, row : row + 16, 128:256] = mixed[quarter * 32 + 16 + slot].astype(BF16)
+                    flat[group, row : row + 16, 128:DEPTH] = mixed[
+                        quarter * 32 + 16 + slot, :, : DEPTH - 128
+                    ].astype(BF16)
             return 0
 
         lax.fori_loop(0, blocks // 16, body, 0)
 
     def turned(rows):
-        return dot_rows(identity[...], rows).astype(BF16)
+        return dot_rows(identity[: rows.shape[1], : rows.shape[1]], rows).astype(BF16)
 
     def prepare_lower(piece, _):
         flatten_piece(piece)
 
         def body(group, _):
-            mats[piece * groups + group] = turned(flat[group])
+            mats[piece * groups + group] = turned(flat[group, :, :DEPTH])
             return 0
 
         lax.fori_loop(0, groups, body, 0, unroll=4)
@@ -199,7 +201,7 @@
                 jnp.where(member_lane == member, inverses, jnp.zeros_like(inverses))
                 for member in range(GROUP)
             ]
-            product = dot_rows(turned(flat[group]), jnp.concatenate(apart, axis=0))
+            product = dot_rows(turned(flat[group, :, :DEPTH]), jnp.concatenate(apart, axis=0))
             mats[piece * groups + group] = product.astype(BF16)
             return 0
 
@@ -216,7 +218,7 @@
                 rhs[color, first + slot] = doubled(lines[slot])
             return 0
 
-        lax.fori_loop(0, colors * blocks // 8, body, 0, unroll=2)
+        lax.fori_loop(0, colors * blocks // 8, body, 0, unroll=8)
 
     def prepare_sums():
         load_dinv.wait()
@@ -301,7 +303,9 @@
         members = []
         for member in range(GROUP):
             first, second, third = [source[at] for at in indices(group * GROUP + member)]
-            members.append(jnp.concatenate([jnp.where(low_half16, first, second), third], axis=1))
+            members.append(
+                jnp.concatenate([jnp.where(low_half16, first, second), third[:, :BS]], axis=1)
+            )
         return jnp.concatenate(members, axis=0)
 
     def own_block(product, member):
@@ -359,7 +363,7 @@
         def color_body(color, _):
             flatten_piece(color - 1)
             forward_step(
-                lambda rows, group: dot_rows(rows, flat[group]),
+                lambda rows, group: dot_rows(rows, flat[group, :, :DEPTH]),
                 lower_indices(color),
                 solved.at[color - 1],
                 color,
@@ -461,13 +465,10 @@
     lax.fori_loop(0, steps, scale_solved, 0)
 
     def store_out(color):
-        def body(group, _):
-            values = [paired(table[color, group * GROUP + member].astype(F32)) for member in range(GROUP)]
-            at = pl.ds(pl.multiple_of(group * GROUP * 8, GROUP * 8), GROUP * 8)
-            out[color, at, :] = jnp.concatenate(values, axis=0).astype(BF16)
-            return 0
-
-        lax.fori_loop(0, groups, body, 0, unroll=4)
+        for first in range(0, blocks, 16):
+            values = [paired(table[color, first + slot].astype(F32))[None] for slot in range(16)]
+            rows = jnp.concatenate(values, axis=0).reshape(16, 16 * BS)
+            out[color, first : first + 16, :] = rows.astype(BF16)
 
     @pl.when(level == levels - 1)
     def _():
@@ -493,6 +494,7 @@
     def back_color(step, _):
         color = colors - 2 - step
         source = table.at[color + 1]
+        store_out(color + 1)
         multiply = by_piece(steps + 1 + color)
 
         def indices(block):
@@ -542,11 +544,7 @@
                 device_id_type=MESH,
             ).start()
 
-    def color_out(color, _):
-        store_out(color)
-        return 0
-
-    lax.fori_loop(0, colors, color_out, 0)
+    store_out(0)
 
     @pl.when(level > 0)
     def _():
@@ -582,7 +580,7 @@
     hbm = pl.BlockSpec(memory_space=pl.ANY)
     answer = pl.pallas_call(
         functools.partial(kernel, levels, parts),
-        out_shape=jax.ShapeDtypeStruct((colors, blocks * 8, 128), BF16),
+        out_shape=jax.ShapeDtypeStruct((colors, blocks, features), BF16),
         in_specs=[smem] * 4 + [hbm] * 6,
         out_specs=vmem,
         scratch_shapes=[
@@ -591,7 +589,7 @@
             pltpu.VMEM((3, blocks, entries), BF16),
             pltpu.VMEM((colors, blocks, entries), BF16),
             pltpu.VMEM((groups, GROUP * BS, 256), BF16),
-            pltpu.VMEM((pieces * groups, 256, GROUP * BS), BF16),
+            pltpu.VMEM((pieces * groups, DEPTH, GROUP * BS), BF16),
             pltpu.VMEM((groups, GROUP * BS, 256), BF16),
             pltpu.VMEM((colors * groups, BS, GROUP * BS), BF16),
             pltpu.VMEM((colors * groups, GROUP * BS, 2 * BS), BF16),
@@ -633,7 +631,7 @@
         jnp.swapaxes(upper_remote, 2, 3),
         dinv,
     )
-    return answer.reshape(1, 1, colors, blocks, features)
+    return answer[None, None]
 
 
 def solution(mesh):

time: 92.7 us -> 91.2 us (0.984)
  Pallas kernels: 90.4 us -> 89.2 us
    reshape x1 -> x0, local copies, waits for them, and re-layouts: 2.06 us -> none  [per_device(): return answer.reshape(1, 1, colors, blocks, features)]
    unnamed x0 -> x1, local copies, waits for them, and re-layouts: none -> 1.87 us
    pallas_call x1, Pallas kernels: 90.4 us -> 89.2 us  [per_device(): pl.pallas_call(functools.partial(kernel, levels, parts), out_shape=jax.Sh...]
where the time goes in v5:
time: 91.2 us; the launch traced here: 91.1 us
  Pallas kernels  89.2 us (98%)
  local copies, waits for them, and re-layouts  1.87 us (2%)
    pallas_call x1, Pallas kernels, per_device(): pl.pallas_call(functools.partial(kernel, levels, parts), out_shape=jax.Sh...  89.2 us
    unnamed x1, local copies, waits for them, and re-layouts  1.87 us

profile of v5, /device:TPU:1, one launch (start us, length us, event | category | flops | bytes accessed | tf_op | source)
XLA Modules:
  0.0 91.1 jit_solution(732086222986572444)
XLA Ops:
  0.0 89.2 %sweeps.1 = bf16[4,64,1024]{2,1,0:T(8,128)(2,1)} custom-call(s32[1,3,3,1,64]{4,3,2,1,0:T(1,128)} %bitcast.16, s32[1,3,3,1,64]{4,3,2,1,0:T(1,128)} %bitcast.17, s32[1,3,1,64]{3,2,1,0:T(1,128)} %bitcast.19, s32[4,32]{1,0:T(4,128)} %bitcast.18, f32[1,1,4,64,1024]{4,3,2,1,0:T(8,128)} %rhs_hbm.1, bf16[1,1,3,3,64,4096]{5,4,3,2,1,0:T(8,128)(2,1)} %bitcast.11, ...), custom_call_target="tpu_custom_call" | custom-call | tf_op jit(solution)/shard_map/sweeps/pallas_call | solution.py:581
  89.2 1.9 %copy.12 = bf16[1,1,4,64,1024]{4,3,2,1,0:T(8,128)(2,1)} copy(bf16[1,1,4,64,1024]{4,3,2,1,0:T(8,128)(2,1)} %bitcast.13) | data formatting | bytes 1048576

commit v6 on v5

--- a/solution.py
+++ b/solution.py
@@ -56,10 +56,8 @@
     mixed,
     solved,
     reduced,
-    base,
     table,
     rtable,
-    boundary,
     upward,
     terms,
     edge_code,
@@ -75,11 +73,11 @@
 ):
     level = lax.axis_index("level")
     me = lax.axis_index("dom")
-    colors, blocks = solved.shape[0], solved.shape[1]
+    colors, blocks = solved.shape[1], solved.shape[2]
     steps = colors - 1
     groups = blocks // GROUP
     per_peer = send_idx.shape[0]
-    rows_per_peer = send_f.shape[0] // parts
+    rows_per_peer = send_f.shape[1] // parts
     offsets, sides = far_first(parts)
     at_z, at_y, at_core = me // (sides[1] * sides[2]), lax.rem(me // sides[2], sides[1]), lax.rem(me, sides[2])
     peers = [
@@ -125,18 +123,9 @@
 
     lax.fori_loop(0, parts, greet, 0)
 
-    low_half16 = lax.broadcasted_iota(jnp.int32, (16, 128), 1) < BS
     low_half8 = lax.broadcasted_iota(jnp.int32, (8, 128), 1) < BS
-    zero16 = jnp.zeros((16, 128), BF16)
-
-    def doubled(packed):
-        turned = pltpu.roll(packed, BS, 1)
-        return jnp.concatenate(
-            [jnp.where(low_half8, packed, turned), jnp.where(low_half8, turned, packed)], axis=0
-        )
-
-    def paired(rows):
-        return jnp.where(low_half8, rows[:8], rows[8:])
+    top_half8 = lax.broadcasted_iota(jnp.int32, (8, 128), 0) < 4
+    zero8 = jnp.zeros((8, 128), F32)
 
     def interleave(slot, first, second):
         first_turned = pltpu.roll(first, BS, 1)
@@ -152,7 +141,7 @@
     def await_piece(piece):
         pltpu.make_async_copy(lrem_hbm.at[0, 0], raw.at[piece], load_sems.at[piece]).wait()
 
-    def flatten_piece(piece):
+    def flatten_piece(piece, target):
         await_piece(piece)
 
         def body(step, _):
@@ -166,7 +155,7 @@
                     mixed[at, pl.ds(0, 8, stride=2), :] = third
                     mixed[at, pl.ds(1, 8, stride=2), :] = turned
                 for slot in range(16):
-                    group = step * GROUP + slot // GROUP
+                    group = target * groups + step * GROUP + slot // GROUP
                     row = (slot % GROUP) * BS + quarter * 16
                     flat[group, row : row + 16, 0:128] = mixed[quarter * 32 + slot].astype(BF16)
                     flat[group, row : row + 16, 128:DEPTH] = mixed[
@@ -180,7 +169,7 @@
         return dot_rows(identity[: rows.shape[1], : rows.shape[1]], rows).astype(BF16)
 
     def prepare_lower(piece, _):
-        flatten_piece(piece)
+        flatten_piece(piece, 0)
 
         def body(group, _):
             mats[piece * groups + group] = turned(flat[group, :, :DEPTH])
@@ -193,7 +182,7 @@
 
     def prepare_upper(color, _):
         piece = steps + 1 + color
-        flatten_piece(piece)
+        flatten_piece(piece, 0)
 
         def body(group, _):
             inverses = w_dinv[color * groups + group]
@@ -215,7 +204,12 @@
             color, first = step // (blocks // 8), lax.rem(step, blocks // 8) * 8
             lines = raw_rhs[color, pl.ds(pl.multiple_of(first, 8), 8), :].reshape(8, 8, 128)
             for slot in range(8):
-                rhs[color, first + slot] = doubled(lines[slot])
+                line = lines[slot]
+                turn = pltpu.roll(line, BS, 1)
+                even = jnp.where(low_half8, line, turn)
+                odd = pltpu.roll(jnp.where(low_half8, turn, line), 4, 0)
+                rhs[0, color, first + slot] = jnp.where(top_half8, even, odd)
+                rhs[1, color, first + slot] = jnp.where(top_half8, odd, even)
             return 0
 
         lax.fori_loop(0, colors * blocks // 8, body, 0, unroll=8)
@@ -271,20 +265,29 @@
         lax.fori_loop(0, groups, urem_turn, 0, unroll=4)
 
         lane = lax.broadcasted_iota(jnp.int32, (8, 128), 1)
-        for vector in range(edge_code.shape[1] // 128):
+
+        def spell(number_of):
             code = jnp.zeros((8, 128), jnp.int32)
             for within in range(16):
-                edge = vector * 16 + within
-                code = jnp.where(lane // 8 == within, slot_idx[0, edge % 3, 0, edge // 3] * 8 + lane % 8, code)
-            edge_code[:, vector * 128 : vector * 128 + 128] = code
-        for vector in range(owner_code.shape[1] // 128):
-            code = jnp.zeros((8, 128), jnp.int32)
-            for within in range(16):
-                slot = vector * 16 + within
-                code = jnp.where(
-                    lane // 8 == within, send_idx[slot % per_peer, slot // per_peer] * 8 + lane % 8, code
-                )
-            owner_code[:, vector * 128 : vector * 128 + 128] = code
+                code = jnp.where(lane // 8 == within, number_of(within), code)
+            return code
+
+        per_term = blocks // 16
+        for parity, couples in enumerate(((0, 1, 2), (1, 0, 2))):
+            for vector in range(3 * per_term):
+                couple, first = couples[vector // per_term], vector % per_term * 16
+                slot = spell(lambda within: slot_idx[0, couple, 0, first + within])
+                place = jnp.where(slot % 2 == parity, slot // 2 * 8 + lane % 8, -1)
+                edge_code[parity, :, vector * 128 : vector * 128 + 128] = place
+            for vector in range(owner_code.shape[2] // 128):
+                pairs = per_peer // 2
+
+                def owner(within):
+                    at = vector * 16 + within
+                    return send_idx[at % pairs * 2 + parity, at // pairs]
+
+                place = spell(owner) * 8 + lane % 8
+                owner_code[parity, :, vector * 128 : vector * 128 + 128] = place
 
         def hot(target, codes):
             def body(chunk, _):
@@ -296,48 +299,49 @@
 
             lax.fori_loop(0, target.shape[0] // 64, body, 0)
 
-        hot(edge_hot, edge_code)
-        hot(owner_hot, owner_code)
+        for parity in range(2):
+            hot(edge_hot.at[parity], edge_code.at[parity])
+            hot(owner_hot.at[parity], owner_code.at[parity])
 
     def gathered(indices, source, group):
-        members = []
+        firsts, thirds = [], []
         for member in range(GROUP):
             first, second, third = [source[at] for at in indices(group * GROUP + member)]
-            members.append(
-                jnp.concatenate([jnp.where(low_half16, first, second), third[:, :BS]], axis=1)
-            )
-        return jnp.concatenate(members, axis=0)
+            firsts.append(jnp.where(low_half8, first, second))
+            thirds.append(third)
+        third = jnp.concatenate(thirds, axis=0)[:, :BS]
+        return jnp.concatenate([jnp.concatenate(firsts, axis=0), third], axis=1).astype(BF16)
 
     def own_block(product, member):
         lanes = slice((member // 2) * 128, (member // 2) * 128 + 128)
-        piece = product[member * 16 : member * 16 + 16, lanes]
-        turned = pltpu.roll(piece, BS, 1)
+        piece = product[member * 8 : member * 8 + 8, lanes]
+        turn = pltpu.roll(piece, BS, 1)
         if member % 2 == 0:
-            return jnp.where(low_half16, piece, turned)
-        return jnp.where(low_half16, turned, piece)
+            return jnp.where(low_half8, piece, turn)
+        return jnp.where(low_half8, turn, piece)
 
     def spread(source, group):
         members = []
         for member in range(GROUP):
             value = source[group * GROUP + member]
             if member % 2 == 0:
-                kept = jnp.where(low_half16, value, zero16)
+                kept = jnp.where(low_half8, value, zero8)
             else:
-                kept = jnp.where(low_half16, zero16, value)
-            pair = [kept, zero16] if member < 2 else [zero16, kept]
+                kept = jnp.where(low_half8, zero8, value)
+            pair = [kept, zero8] if member < 2 else [zero8, kept]
             members.append(jnp.concatenate(pair, axis=1))
-        return jnp.concatenate(members, axis=0)
-
-    def forward_step(multiply, indices, source, color):
+        return jnp.concatenate(members, axis=0).astype(BF16)
+
+    def forward_step(multiply, indices, source, half, color):
         def body(group, _):
             product = multiply(gathered(indices, source, group), group)
             for member in range(GROUP):
                 block = group * GROUP + member
-                reduced[block] = (rhs[color, block] - own_block(product, member)).astype(BF16)
+                reduced[block] = rhs[half, color, block] - own_block(product, member)
             return 0
 
         lax.fori_loop(0, groups, body, 0, unroll=groups)
-        solved[color] = reduced[...]
+        solved[half, color] = reduced[...]
 
     def by_piece(piece):
         return lambda rows, group: jnp.dot(
@@ -354,23 +358,7 @@
 
     @pl.when(level == 0)
     def _():
-        def body(block, _):
-            solved[0, block] = rhs[0, block].astype(BF16)
-            return 0
-
-        lax.fori_loop(0, blocks, body, 0, unroll=8)
-
-        def color_body(color, _):
-            flatten_piece(color - 1)
-            forward_step(
-                lambda rows, group: dot_rows(rows, flat[group, :, :DEPTH]),
-                lower_indices(color),
-                solved.at[color - 1],
-                color,
-            )
-            return 0
-
-        lax.fori_loop(1, colors, color_body, 0)
+        flatten_piece(0, 0)
 
     identity[...] = jnp.where(
         lax.broadcasted_iota(jnp.int32, (256, 256), 0) == lax.broadcasted_iota(jnp.int32, (256, 256), 1),
@@ -388,51 +376,78 @@
 
     lax.fori_loop(0, jnp.where(level == levels - 1, steps, 0), prepare_upper, 0)
 
-    @pl.when(level > 0)
-    def _():
-        pltpu.make_async_copy(recv_f, recv_f, sems.at[1]).wait()
-
-        def body(pair, _):
-            both = recv_f[pl.ds(pl.multiple_of(pair * 16, 16), 16), :].astype(F32)
-            rtable[pair * 2] = doubled(both[:8]).astype(BF16)
-            rtable[pair * 2 + 1] = doubled(both[8:]).astype(BF16)
-            return 0
-
-        lax.fori_loop(0, recv_f.shape[0] // 16, body, 0, unroll=8)
-        forward_step(by_piece(remote_piece), remote_indices, rtable, 0)
-
-        def color_body(color, _):
-            forward_step(by_piece(color - 1), lower_indices(color), solved.at[color - 1], color)
-            return 0
-
-        lax.fori_loop(1, colors, color_body, 0)
-
     pl.semaphore_wait(
         barrier, parts * ((level > 0).astype(jnp.int32) + (level < levels - 1).astype(jnp.int32))
     )
 
-    @pl.when(level < levels - 1)
-    def _():
-        def pack(block, _):
-            boundary[block] = paired(solved[colors - 1, block].astype(F32))
-            return 0
-
-        lax.fori_loop(0, blocks, pack, 0, unroll=8)
-
-        for peer in peers:
-            for pair in range(per_peer // 2):
-                both = jnp.concatenate(
-                    [boundary[send_idx[pair * 2, peer]], boundary[send_idx[pair * 2 + 1, peer]]], axis=0
+    def peer_rows(peer):
+        return pl.ds(pl.multiple_of(peer * rows_per_peer, 16), rows_per_peer)
+
+    def forward_half(half, _):
+        @pl.when(level == 0)
+        def _():
+            solved[half, 0] = rhs[half, 0]
+
+            def color_body(color, _):
+                @pl.when((half == 0) & (color > 1))
+                def _():
+                    flatten_piece(color - 1, color - 1)
+
+                forward_step(
+                    lambda rows, group: dot_rows(rows, flat[(color - 1) * groups + group, :, :DEPTH]),
+                    lower_indices(color),
+                    solved.at[half, color - 1],
+                    half,
+                    color,
                 )
-                send_f[pl.ds(pl.multiple_of(peer * rows_per_peer + pair * 16, 16), 16), :] = both.astype(BF16)
-            pltpu.make_async_remote_copy(
-                src_ref=send_f.at[pl.ds(pl.multiple_of(peer * rows_per_peer, 16), rows_per_peer)],
-                dst_ref=recv_f.at[pl.ds(pl.multiple_of(me * rows_per_peer, 16), rows_per_peer)],
-                send_sem=sems.at[0],
-                recv_sem=sems.at[1],
-                device_id=(level + 1, peer),
-                device_id_type=MESH,
-            ).start()
+                return 0
+
+            lax.fori_loop(1, colors, color_body, 0)
+
+        @pl.when(level > 0)
+        def _():
+            pltpu.make_async_copy(recv_f.at[half], recv_f.at[half], sems.at[2 + half]).wait()
+
+            def body(pair, _):
+                both = recv_f[half, pl.ds(pl.multiple_of(pair * 16, 16), 16), :].astype(F32)
+                for side in range(2):
+                    line = both[side * 8 : side * 8 + 8]
+                    turn = pltpu.roll(line, BS, 1)
+                    rtable[pair * 4 + side * 2] = jnp.where(low_half8, line, turn)
+                    rtable[pair * 4 + side * 2 + 1] = jnp.where(low_half8, turn, line)
+                return 0
+
+            lax.fori_loop(0, recv_f.shape[1] // 16, body, 0, unroll=8)
+            forward_step(by_piece(remote_piece), remote_indices, rtable, half, 0)
+
+            def color_body(color, _):
+                forward_step(
+                    by_piece(color - 1), lower_indices(color), solved.at[half, color - 1], half, color
+                )
+                return 0
+
+            lax.fori_loop(1, colors, color_body, 0)
+
+        @pl.when(level < levels - 1)
+        def _():
+            for peer in peers:
+                lines = []
+                for pair in range(per_peer // 2):
+                    even, odd = reduced[send_idx[pair * 2, peer]], reduced[send_idx[pair * 2 + 1, peer]]
+                    lines.append(jnp.where(low_half8, even, odd))
+                send_f[half, peer_rows(peer), :] = jnp.concatenate(lines, axis=0).astype(BF16)
+                pltpu.make_async_remote_copy(
+                    src_ref=send_f.at[half, peer_rows(peer)],
+                    dst_ref=recv_f.at[half, peer_rows(me)],
+                    send_sem=sems.at[half],
+                    recv_sem=sems.at[2 + half],
+                    device_id=(level + 1, peer),
+                    device_id_type=MESH,
+                ).start()
+
+        return 0
+
+    lax.fori_loop(0, 2, forward_half, 0)
 
     @pl.when(level == 0)
     def _():
@@ -450,109 +465,122 @@
                 spread(source, group), mat_dinv[color * groups + group], preferred_element_type=F32
             )
             for member in range(GROUP):
-                put(group * GROUP + member, product[member * 16 : member * 16 + 16])
+                put(group * GROUP + member, product[member * 8 : member * 8 + 8])
             return 0
 
         lax.fori_loop(0, groups, body, 0, unroll=groups)
 
-    def scale_solved(color, _):
+    def scale_solved(at, _):
+        half, color = at // steps, lax.rem(at, steps)
+
         def put(block, value):
-            base[color, block] = value
-
-        scale(color, solved.at[color], put)
+            rhs[half, color, block] = value
+
+        scale(color, solved.at[half, color], put)
         return 0
 
-    lax.fori_loop(0, steps, scale_solved, 0)
+    lax.fori_loop(0, 2 * steps, scale_solved, 0)
 
     def store_out(color):
         for first in range(0, blocks, 16):
-            values = [paired(table[color, first + slot].astype(F32))[None] for slot in range(16)]
+            values = []
+            for slot in range(16):
+                zero_half, one_half = table[0, color, first + slot], table[1, color, first + slot]
+                even = jnp.where(top_half8, zero_half, one_half)
+                odd = pltpu.roll(jnp.where(top_half8, one_half, zero_half), 4, 0)
+                values.append(jnp.where(low_half8, even, odd)[None])
             rows = jnp.concatenate(values, axis=0).reshape(16, 16 * BS)
             out[color, first : first + 16, :] = rows.astype(BF16)
 
-    @pl.when(level == levels - 1)
-    def _():
-        upward[...] = jnp.zeros_like(upward)
-
-    @pl.when(level < levels - 1)
-    def _():
-        pltpu.make_async_copy(recv_b, recv_b, sems.at[3]).wait()
-        upward[...] = jnp.dot(owner_hot[...], recv_b[...], preferred_element_type=F32)
-
-    def last_color(block, _):
-        add = doubled(upward[pl.ds(pl.multiple_of(block * 8, 8), 8), :])
-        reduced[block] = (solved[colors - 1, block].astype(F32) - add).astype(BF16)
+    low_lanes = lax.broadcasted_iota(jnp.int32, upward.shape, 1) < BS
+    low_sums = lax.broadcasted_iota(jnp.int32, send_b.shape[1:], 1) < BS
+
+    def backward_half(half, _):
+        @pl.when(level == levels - 1)
+        def _():
+            upward[...] = jnp.zeros_like(upward)
+
+        @pl.when(level < levels - 1)
+        def _():
+            pltpu.make_async_copy(recv_b.at[half], recv_b.at[half], sems.at[6 + half]).wait()
+            even = jnp.dot(owner_hot[0], recv_b[half], preferred_element_type=F32)
+            odd = jnp.dot(owner_hot[1], recv_b[half], preferred_element_type=F32)
+            upward[...] = jnp.where(low_lanes, even, odd)
+
+        def last_color(block, _):
+            parts_of = upward[pl.ds(pl.multiple_of(block * 8, 8), 8), :]
+            reduced[block] = solved[half, colors - 1, block] - (parts_of + pltpu.roll(parts_of, BS, 1))
+            return 0
+
+        lax.fori_loop(0, blocks, last_color, 0, unroll=16)
+
+        def put_last(block, value):
+            table[half, colors - 1, block] = value
+
+        scale(colors - 1, reduced, put_last)
+
+        def back_color(step, _):
+            color = colors - 2 - step
+            source = table.at[half, color + 1]
+            store_out(color + 1)
+            multiply = by_piece(steps + 1 + color)
+
+            def indices(block):
+                return [up_idx[0, color, couple, 0, block] for couple in range(3)]
+
+            def body(group, _):
+                product = multiply(gathered(indices, source, group), group)
+                for member in range(GROUP):
+                    block = group * GROUP + member
+                    reduced[block] = rhs[half, color, block] - own_block(product, member)
+                return 0
+
+            lax.fori_loop(0, groups, body, 0, unroll=groups)
+            table[half, color] = reduced[...]
+            return 0
+
+        lax.fori_loop(0, steps, back_color, 0)
+
+        @pl.when(level > 0)
+        def _():
+            def body(group, _):
+                product = jnp.dot(
+                    spread(reduced, group), mat_urem[group], preferred_element_type=F32
+                )
+                both, third = product[:, :128], product[:, 128:]
+                for term, value in enumerate((both, pltpu.roll(both, BS, 1), third)):
+                    at = term * blocks * 8 + group * GROUP * 8
+                    terms[pl.ds(pl.multiple_of(at, GROUP * 8), GROUP * 8), :] = value.astype(BF16)
+                return 0
+
+            lax.fori_loop(0, groups, body, 0, unroll=groups)
+            even = jnp.dot(edge_hot[0], terms[...], preferred_element_type=F32)
+            odd = jnp.dot(edge_hot[1], terms[...], preferred_element_type=F32)
+            send_b[half] = jnp.where(low_sums, even, odd).astype(BF16)
+            for peer in peers:
+                pltpu.make_async_remote_copy(
+                    src_ref=send_b.at[half, peer_rows(peer)],
+                    dst_ref=recv_b.at[half, peer_rows(me)],
+                    send_sem=sems.at[4 + half],
+                    recv_sem=sems.at[6 + half],
+                    device_id=(level - 1, peer),
+                    device_id_type=MESH,
+                ).start()
+
         return 0
 
-    lax.fori_loop(0, blocks, last_color, 0, unroll=16)
-
-    def put_last(block, value):
-        table[colors - 1, block] = value.astype(BF16)
-
-    scale(colors - 1, reduced, put_last)
-
-    def back_color(step, _):
-        color = colors - 2 - step
-        source = table.at[color + 1]
-        store_out(color + 1)
-        multiply = by_piece(steps + 1 + color)
-
-        def indices(block):
-            return [up_idx[0, color, couple, 0, block] for couple in range(3)]
-
-        def body(group, _):
-            product = multiply(gathered(indices, source, group), group)
-            for member in range(GROUP):
-                block = group * GROUP + member
-                reduced[block] = (base[color, block] - own_block(product, member)).astype(BF16)
-            return 0
-
-        lax.fori_loop(0, groups, body, 0, unroll=groups)
-        table[color] = reduced[...]
-        return 0
-
-    lax.fori_loop(0, steps, back_color, 0)
-
-    @pl.when(level > 0)
-    def _():
-        def body(group, _):
-            product = jnp.dot(
-                spread(table.at[0], group), mat_urem[group], preferred_element_type=F32
-            )
-            results = []
-            for member in range(GROUP):
-                rows = product[member * 16 : member * 16 + 16]
-                both, third = rows[:, :128], rows[:, 128:]
-                turned = pltpu.roll(both, BS, 1)
-                results.append(jnp.where(low_half8, both[:8], turned[8:]))
-                results.append(jnp.where(low_half8, turned[:8], both[8:]))
-                results.append(paired(third))
-            at = pl.ds(pl.multiple_of(group * GROUP * 24, 96), GROUP * 24)
-            terms[at, :] = jnp.concatenate(results, axis=0).astype(BF16)
-            return 0
-
-        lax.fori_loop(0, groups, body, 0, unroll=groups)
-        send_b[...] = jnp.dot(edge_hot[...], terms[...], preferred_element_type=F32).astype(BF16)
-
-        for peer in peers:
-            pltpu.make_async_remote_copy(
-                src_ref=send_b.at[pl.ds(pl.multiple_of(peer * rows_per_peer, 16), rows_per_peer)],
-                dst_ref=recv_b.at[pl.ds(pl.multiple_of(me * rows_per_peer, 16), rows_per_peer)],
-                send_sem=sems.at[2],
-                recv_sem=sems.at[3],
-                device_id=(level - 1, peer),
-                device_id_type=MESH,
-            ).start()
-
+    lax.fori_loop(0, 2, backward_half, 0)
     store_out(0)
 
-    @pl.when(level > 0)
-    def _():
-        pltpu.make_async_copy(send_b, send_b, sems.at[2]).wait()
-
-    @pl.when(level < levels - 1)
-    def _():
-        pltpu.make_async_copy(send_f, send_f, sems.at[0]).wait()
+    for half in range(2):
+
+        @pl.when(level > 0)
+        def _():
+            pltpu.make_async_copy(send_b.at[half], send_b.at[half], sems.at[4 + half]).wait()
+
+        @pl.when(level < levels - 1)
+        def _():
+            pltpu.make_async_copy(send_f.at[half], send_f.at[half], sems.at[half]).wait()
 
 
 def per_device(
@@ -588,31 +616,29 @@
             pltpu.VMEM((pieces, 3, blocks, entries), BF16),
             pltpu.VMEM((3, blocks, entries), BF16),
             pltpu.VMEM((colors, blocks, entries), BF16),
-            pltpu.VMEM((groups, GROUP * BS, 256), BF16),
+            pltpu.VMEM((steps * groups, GROUP * BS, 256), BF16),
             pltpu.VMEM((pieces * groups, DEPTH, GROUP * BS), BF16),
             pltpu.VMEM((groups, GROUP * BS, 256), BF16),
             pltpu.VMEM((colors * groups, BS, GROUP * BS), BF16),
             pltpu.VMEM((colors * groups, GROUP * BS, 2 * BS), BF16),
             pltpu.VMEM((256, 256), BF16),
-            pltpu.VMEM((colors, blocks, 16, 128), F32),
+            pltpu.VMEM((2, colors, blocks, 8, 128), F32),
             pltpu.VMEM((128, 16, 128), F32),
-            pltpu.VMEM((colors, blocks, 16, 128), BF16),
-            pltpu.VMEM((blocks, 16, 128), BF16),
-            pltpu.VMEM((steps, blocks, 16, 128), F32),
-            pltpu.VMEM((colors, blocks, 16, 128), BF16),
-            pltpu.VMEM((slots, 16, 128), BF16),
+            pltpu.VMEM((2, colors, blocks, 8, 128), F32),
             pltpu.VMEM((blocks, 8, 128), F32),
+            pltpu.VMEM((2, colors, blocks, 8, 128), F32),
+            pltpu.VMEM((slots, 8, 128), F32),
             pltpu.VMEM((blocks * 8, 128), F32),
             pltpu.VMEM((blocks * 24, 128), BF16),
-            pltpu.VMEM((8, blocks * 24), jnp.int32),
-            pltpu.VMEM((8, slots * 8), jnp.int32),
-            pltpu.VMEM((slots * 8, blocks * 24), BF16),
-            pltpu.VMEM((blocks * 8, slots * 8), BF16),
-            pltpu.VMEM((slots * 8, 128), BF16),
-            pltpu.VMEM((slots * 8, 128), BF16),
-            pltpu.VMEM((slots * 8, 128), BF16),
-            pltpu.VMEM((slots * 8, 128), BF16),
-            pltpu.SemaphoreType.DMA((4,)),
+            pltpu.VMEM((2, 8, blocks * 24), jnp.int32),
+            pltpu.VMEM((2, 8, slots * 4), jnp.int32),
+            pltpu.VMEM((2, slots * 4, blocks * 24), BF16),
+            pltpu.VMEM((2, blocks * 8, slots * 4), BF16),
+            pltpu.VMEM((2, slots * 4, 128), BF16),
+            pltpu.VMEM((2, slots * 4, 128), BF16),
+            pltpu.VMEM((2, slots * 4, 128), BF16),
+            pltpu.VMEM((2, slots * 4, 128), BF16),
+            pltpu.SemaphoreType.DMA((8,)),
             pltpu.SemaphoreType.DMA((pieces + 3,)),
         ],
         compiler_params=pltpu.CompilerParams(

time: 91.2 us -> 88.7 us (0.973)
  Pallas kernels: 89.2 us -> 86.6 us
    pallas_call x1, Pallas kernels: 89.2 us -> 86.6 us  [per_device(): pl.pallas_call(functools.partial(kernel, levels, parts), out_shape=jax.Sh...]
where the time goes in v6:
time: 88.7 us; the launch traced here: 88.5 us
  Pallas kernels  86.6 us (98%)
  local copies, waits for them, and re-layouts  1.87 us (2%)
    pallas_call x1, Pallas kernels, per_device(): pl.pallas_call(functools.partial(kernel, levels, parts), out_shape=jax.Sh...  86.6 us
    unnamed x1, local copies, waits for them, and re-layouts  1.87 us

profile of v6, /device:TPU:1, one launch (start us, length us, event | category | flops | bytes accessed | tf_op | source)
XLA Modules:
  0.0 88.5 jit_solution(2686389090448703713)
XLA Ops:
  0.0 86.6 %sweeps.1 = bf16[4,64,1024]{2,1,0:T(8,128)(2,1)} custom-call(s32[1,3,3,1,64]{4,3,2,1,0:T(1,128)} %bitcast.16, s32[1,3,3,1,64]{4,3,2,1,0:T(1,128)} %bitcast.17, s32[1,3,1,64]{3,2,1,0:T(1,128)} %bitcast.19, s32[4,32]{1,0:T(4,128)} %bitcast.18, f32[1,1,4,64,1024]{4,3,2,1,0:T(8,128)} %rhs_hbm.1, bf16[1,1,3,3,64,4096]{5,4,3,2,1,0:T(8,128)(2,1)} %bitcast.11, ...), custom_call_target="tpu_custom_call" | custom-call | tf_op jit(solution)/shard_map/sweeps/pallas_call | solution.py:609
  86.6 1.9 %copy.12 = bf16[1,1,4,64,1024]{4,3,2,1,0:T(8,128)(2,1)} copy(bf16[1,1,4,64,1024]{4,3,2,1,0:T(8,128)(2,1)} %bitcast.13) | data formatting | bytes 1048576

commit v7 on v6

--- a/solution.py
+++ b/solution.py
@@ -301,7 +301,11 @@
 
         for parity in range(2):
             hot(edge_hot.at[parity], edge_code.at[parity])
-            hot(owner_hot.at[parity], owner_code.at[parity])
+
+        @pl.when(level < levels - 1)
+        def _():
+            for parity in range(2):
+                hot(owner_hot.at[parity], owner_code.at[parity])
 
     def gathered(indices, source, group):
         firsts, thirds = [], []
@@ -366,15 +370,12 @@
         0.0,
     ).astype(BF16)
 
-    @pl.when(level > 0)
-    def _():
-        lax.fori_loop(0, steps + 1, prepare_lower, 0)
+    ahead = jnp.where(level == 0, 0, jnp.where(level == levels - 1, pieces, steps + 1))
+    lax.fori_loop(0, ahead, prepare_lower, 0)
 
     @pl.when(level >= 2)
     def _():
         prepare_sums()
-
-    lax.fori_loop(0, jnp.where(level == levels - 1, steps, 0), prepare_upper, 0)
 
     pl.semaphore_wait(
         barrier, parts * ((level > 0).astype(jnp.int32) + (level < levels - 1).astype(jnp.int32))
@@ -479,7 +480,16 @@
         scale(color, solved.at[half, color], put)
         return 0
 
-    lax.fori_loop(0, 2 * steps, scale_solved, 0)
+    @pl.when(level < levels - 1)
+    def _():
+        lax.fori_loop(0, 2 * steps, scale_solved, 0)
+
+    @pl.when(level == levels - 1)
+    def _():
+        for half in range(2):
+            for color in range(steps):
+                rhs[half, color] = solved[half, color]
+
 
     def store_out(color):
         for first in range(0, blocks, 16):
@@ -498,7 +508,7 @@
     def backward_half(half, _):
         @pl.when(level == levels - 1)
         def _():
-            upward[...] = jnp.zeros_like(upward)
+            reduced[...] = solved[half, colors - 1]
 
         @pl.when(level < levels - 1)
         def _():
@@ -507,12 +517,12 @@
             odd = jnp.dot(owner_hot[1], recv_b[half], preferred_element_type=F32)
             upward[...] = jnp.where(low_lanes, even, odd)
 
-        def last_color(block, _):
-            parts_of = upward[pl.ds(pl.multiple_of(block * 8, 8), 8), :]
-            reduced[block] = solved[half, colors - 1, block] - (parts_of + pltpu.roll(parts_of, BS, 1))
-            return 0
-
-        lax.fori_loop(0, blocks, last_color, 0, unroll=16)
+            def last_color(block, _):
+                parts_of = upward[pl.ds(pl.multiple_of(block * 8, 8), 8), :]
+                reduced[block] = solved[half, colors - 1, block] - (parts_of + pltpu.roll(parts_of, BS, 1))
+                return 0
+
+            lax.fori_loop(0, blocks, last_color, 0, unroll=blocks)
 
         def put_last(block, value):
             table[half, colors - 1, block] = value
@@ -536,7 +546,18 @@
                 return 0
 
             lax.fori_loop(0, groups, body, 0, unroll=groups)
-            table[half, color] = reduced[...]
+
+            @pl.when(level < levels - 1)
+            def _():
+                table[half, color] = reduced[...]
+
+            @pl.when(level == levels - 1)
+            def _():
+                def put(block, value):
+                    table[half, color, block] = value
+
+                scale(color, reduced, put)
+
             return 0
 
         lax.fori_loop(0, steps, back_color, 0)
@@ -545,7 +566,7 @@
         def _():
             def body(group, _):
                 product = jnp.dot(
-                    spread(reduced, group), mat_urem[group], preferred_element_type=F32
+                    spread(table.at[half, 0], group), mat_urem[group], preferred_element_type=F32
                 )
                 both, third = product[:, :128], product[:, 128:]
                 for term, value in enumerate((both, pltpu.roll(both, BS, 1), third)):

time: 88.7 us -> 83.8 us (0.945)
  Pallas kernels: 86.6 us -> 81.8 us
    pallas_call x1, Pallas kernels: 86.6 us -> 81.8 us  [per_device(): pl.pallas_call(functools.partial(kernel, levels, parts), out_shape=jax.Sh...]
where the time goes in v7:
time: 83.8 us; the launch traced here: 83.6 us
  Pallas kernels  81.8 us (98%)
  local copies, waits for them, and re-layouts  1.87 us (2%)
    pallas_call x1, Pallas kernels, per_device(): pl.pallas_call(functools.partial(kernel, levels, parts), out_shape=jax.Sh...  81.8 us
    unnamed x1, local copies, waits for them, and re-layouts  1.87 us

profile of v7, /device:TPU:1, one launch (start us, length us, event | category | flops | bytes accessed | tf_op | source)
XLA Modules:
  0.0 83.6 jit_solution(6781968260537825293)
XLA Ops:
  0.0 81.8 %sweeps.1 = bf16[4,64,1024]{2,1,0:T(8,128)(2,1)} custom-call(s32[1,3,3,1,64]{4,3,2,1,0:T(1,128)} %bitcast.16, s32[1,3,3,1,64]{4,3,2,1,0:T(1,128)} %bitcast.17, s32[1,3,1,64]{3,2,1,0:T(1,128)} %bitcast.19, s32[4,32]{1,0:T(4,128)} %bitcast.18, f32[1,1,4,64,1024]{4,3,2,1,0:T(8,128)} %rhs_hbm.1, bf16[1,1,3,3,64,4096]{5,4,3,2,1,0:T(8,128)(2,1)} %bitcast.11, ...), custom_call_target="tpu_custom_call" | custom-call | tf_op jit(solution)/shard_map/sweeps/pallas_call | solution.py:630
  81.8 1.9 %copy.12 = bf16[1,1,4,64,1024]{4,3,2,1,0:T(8,128)(2,1)} copy(bf16[1,1,4,64,1024]{4,3,2,1,0:T(8,128)(2,1)} %bitcast.13) | data formatting | bytes 1048576

commit v8 on v7

--- a/solution.py
+++ b/solution.py
@@ -99,12 +99,15 @@
     load_urem = pltpu.make_async_copy(urem_hbm.at[0, 0], raw_urem, load_sems.at[pieces + 1])
     load_dinv = pltpu.make_async_copy(dinv_hbm.at[0, 0], raw_dinv, load_sems.at[pieces + 2])
     load_rhs.start()
-    for piece in range(steps + 1):
-        pltpu.make_async_copy(piece_source(piece), raw.at[piece], load_sems.at[piece]).start()
-    load_dinv.start()
-    load_urem.start()
-    for piece in range(steps + 1, pieces):
-        pltpu.make_async_copy(piece_source(piece), raw.at[piece], load_sems.at[piece]).start()
+    pltpu.make_async_copy(piece_source(0), raw.at[0], load_sems.at[0]).start()
+
+    def start_loads():
+        for piece in range(1, steps + 1):
+            pltpu.make_async_copy(piece_source(piece), raw.at[piece], load_sems.at[piece]).start()
+        load_dinv.start()
+        load_urem.start()
+        for piece in range(steps + 1, pieces):
+            pltpu.make_async_copy(piece_source(piece), raw.at[piece], load_sems.at[piece]).start()
 
     barrier = pltpu.get_barrier_semaphore()
 
@@ -175,7 +178,7 @@
             mats[piece * groups + group] = turned(flat[group, :, :DEPTH])
             return 0
 
-        lax.fori_loop(0, groups, body, 0, unroll=4)
+        lax.fori_loop(0, groups, body, 0, unroll=groups)
         return 0
 
     member_lane = lax.broadcasted_iota(jnp.int32, (BS, GROUP * BS), 1) // BS
@@ -199,6 +202,7 @@
 
     def prepare_rhs():
         load_rhs.wait()
+        start_loads()
 
         def body(step, _):
             color, first = step // (blocks // 8), lax.rem(step, blocks // 8) * 8
@@ -237,7 +241,7 @@
             mat_dinv[group] = turned(jnp.concatenate([inverses, inverses], axis=0))
             return 0
 
-        lax.fori_loop(0, colors * groups, dinv_turn, 0, unroll=4)
+        lax.fori_loop(0, colors * groups, dinv_turn, 0, unroll=groups)
         load_urem.wait()
 
         def urem_body(step, _):
@@ -262,7 +266,7 @@
             mat_urem[group] = turned(flat[group])
             return 0
 
-        lax.fori_loop(0, groups, urem_turn, 0, unroll=4)
+        lax.fori_loop(0, groups, urem_turn, 0, unroll=groups)
 
         lane = lax.broadcasted_iota(jnp.int32, (8, 128), 1)
 

time: 83.8 us -> 82.6 us (0.986)
  Pallas kernels: 81.8 us -> 80.5 us
    pallas_call x1, Pallas kernels: 81.8 us -> 80.5 us  [per_device(): pl.pallas_call(functools.partial(kernel, levels, parts), out_shape=jax.Sh...]
where the time goes in v8:
time: 82.6 us; the launch traced here: 82.4 us
  Pallas kernels  80.5 us (97%)
  local copies, waits for them, and re-layouts  1.87 us (2%)
    pallas_call x1, Pallas kernels, per_device(): pl.pallas_call(functools.partial(kernel, levels, parts), out_shape=jax.Sh...  80.5 us
    unnamed x1, local copies, waits for them, and re-layouts  1.87 us

profile of v8, /device:TPU:1, one launch (start us, length us, event | category | flops | bytes accessed | tf_op | source)
XLA Modules:
  0.0 82.4 jit_solution(6131620352574042587)
XLA Ops:
  0.0 80.5 %sweeps.1 = bf16[4,64,1024]{2,1,0:T(8,128)(2,1)} custom-call(s32[1,3,3,1,64]{4,3,2,1,0:T(1,128)} %bitcast.16, s32[1,3,3,1,64]{4,3,2,1,0:T(1,128)} %bitcast.17, s32[1,3,1,64]{3,2,1,0:T(1,128)} %bitcast.19, s32[4,32]{1,0:T(4,128)} %bitcast.18, f32[1,1,4,64,1024]{4,3,2,1,0:T(8,128)} %rhs_hbm.1, bf16[1,1,3,3,64,4096]{5,4,3,2,1,0:T(8,128)(2,1)} %bitcast.11, ...), custom_call_target="tpu_custom_call" | custom-call | tf_op jit(solution)/shard_map/sweeps/pallas_call | solution.py:634
  80.5 1.9 %copy.12 = bf16[1,1,4,64,1024]{4,3,2,1,0:T(8,128)(2,1)} copy(bf16[1,1,4,64,1024]{4,3,2,1,0:T(8,128)(2,1)} %bitcast.13) | data formatting | bytes 1048576

commit v9 on v8

--- a/solution.py
+++ b/solution.py
@@ -166,7 +166,7 @@
                     ].astype(BF16)
             return 0
 
-        lax.fori_loop(0, blocks // 16, body, 0)
+        lax.fori_loop(0, blocks // 16, body, 0, unroll=4)
 
     def turned(rows):
         return dot_rows(identity[: rows.shape[1], : rows.shape[1]], rows).astype(BF16)

time: 82.6 us -> 82 us (level)
  no operation moved by 1% of the time
where the time goes in v9:
time: 82 us; the launch traced here: 81.9 us
  Pallas kernels  80 us (98%)
  local copies, waits for them, and re-layouts  1.87 us (2%)
    pallas_call x1, Pallas kernels, per_device(): pl.pallas_call(functools.partial(kernel, levels, parts), out_shape=jax.Sh...  80 us
    unnamed x1, local copies, waits for them, and re-layouts  1.87 us

profile of v9, /device:TPU:1, one launch (start us, length us, event | category | flops | bytes accessed | tf_op | source)
XLA Modules:
  0.0 81.9 jit_solution(11955868518768062955)
XLA Ops:
  0.0 80.0 %sweeps.1 = bf16[4,64,1024]{2,1,0:T(8,128)(2,1)} custom-call(s32[1,3,3,1,64]{4,3,2,1,0:T(1,128)} %bitcast.16, s32[1,3,3,1,64]{4,3,2,1,0:T(1,128)} %bitcast.17, s32[1,3,1,64]{3,2,1,0:T(1,128)} %bitcast.19, s32[4,32]{1,0:T(4,128)} %bitcast.18, f32[1,1,4,64,1024]{4,3,2,1,0:T(8,128)} %rhs_hbm.1, bf16[1,1,3,3,64,4096]{5,4,3,2,1,0:T(8,128)(2,1)} %bitcast.11, ...), custom_call_target="tpu_custom_call" | custom-call | tf_op jit(solution)/shard_map/sweeps/pallas_call | solution.py:634
  80.0 1.9 %copy.12 = bf16[1,1,4,64,1024]{4,3,2,1,0:T(8,128)(2,1)} copy(bf16[1,1,4,64,1024]{4,3,2,1,0:T(8,128)(2,1)} %bitcast.13) | data formatting | bytes 1048576
